TPU v7x, 32 devices: a whole 2x2x4 slice. The times are simulated.
32 devices in a mesh: expert: 8 (over z, x), tensor: 4 (over y, core).
Axes of the slice: x: 2, y: 2, z: 4, core: 2. Of those that a mesh axis runs over, the one named last changes fastest.
Arguments:
- tokens: bfloat16 [8192, 768], P('expert'), may hold values from -6 to 6
- gain_attn: float32 [768], replicated, may hold values from 0.5 to 1.5
- w_qkv: bfloat16 [3, 768, 768], P(None, None, 'tensor'), may hold values from -0.21875 to 0.21875
- w_proj: bfloat16 [768, 768], P('tensor'), may hold values from -3.5 to 3.5
- rel_bias: float32 [12, 32], P('tensor'), may hold values from -1 to 1
- gain_ffn: float32 [768], replicated, may hold values from 0.5 to 1.5
- w_router: bfloat16 [768, 8], replicated, may hold values from -0.109375 to 0.109375
- w_in: bfloat16 [8, 768, 3072], P('expert', None, 'tensor'), may hold values from -0.21875 to 0.21875
- w_out: bfloat16 [8, 3072, 768], P('expert', 'tensor'), may hold values from -1.5 to 1.5
- routes: int32 [8192, 1], P('expert'), may hold values from 0 to 7; in each aligned block of 1024 rows (0 to 1023, 1024 to 2047, ...) at most 192 rows name the same one
- segment_ids: int32 [8, 1024], P('expert'), may hold values from 0 to 3, never falling along the last dimension, each value on 1 to 512 neighbouring positions
- cotangent: bfloat16 [8192, 768], P('expert'), may hold values from -6 to 6
Outputs:
- output: bfloat16 [8192, 768], P('expert')
- grad_input: float32 [8192, 768], P('expert')
- grad_gain_attn: float32 [768], replicated
- grad_qkv: float32 [3, 768, 768], P(None, None, 'tensor')
- grad_proj: float32 [768, 768], P('tensor')
- grad_rel: float32 [12, 32], P('tensor')
- grad_gain_ffn: float32 [768], replicated
- grad_router: float32 [768, 8], replicated
- grad_w_in: float32 [8, 768, 3072], P('expert', None, 'tensor')
- grad_w_out: float32 [8, 3072, 768], P('expert', 'tensor')
Inputs may be any that keep to these rules, and one draw needn't show every extreme that they name: `routes`: among the 1024 tokens of one sequence no expert is named more than 192 times, a bound that some block reaches. `segment_ids`: within each sequence the document numbers never fall, each document has at most 512 positions.
All inputs are finite; a program needn't handle non-finite values.
Results may differ from a plain program's by a relative error of at most 0.017.
Values may be sent and summed in bfloat16 or wider, within the bound.
No kernel may reach another device: no remote copies, remote signals or barrier semaphores. Data moves between devices by JAX's collectives and lax.ppermute only.
A program may use at most 192 MiB of HBM per device.

v0:
```python
import jax
import jax.numpy as jnp
from jax import lax
from jax.sharding import PartitionSpec as P

FAR_LIMITS = (12, 16, 23, 32, 46, 64, 91)
HIGH = lax.Precision.HIGHEST


def bucket_of(offset):
    distance = jnp.abs(offset)
    far_bucket = jnp.full_like(distance, 8)
    for limit in FAR_LIMITS:
        far_bucket = far_bucket + (distance >= limit).astype(jnp.int32)
    near_far = jnp.where(distance < 8, distance, far_bucket)
    return near_far + 16 * (offset > 0).astype(jnp.int32)


def norm_rows(values, gain):
    return values * lax.rsqrt(jnp.mean(values * values, -1, keepdims=True) + 1e-06) * gain


def send_rows(rows, table, experts, capacity):
    groups = lax.axis_size("expert")
    width = rows.shape[1]
    outgoing = jnp.einsum("te,td->ed", table, rows, preferred_element_type=jnp.float32).astype(
        jnp.bfloat16
    )
    outgoing = outgoing.reshape(groups, experts // groups, capacity, width)
    return lax.all_to_all(outgoing, "expert", split_axis=0, concat_axis=0, tiled=True)


def take_back(partial_value, table, experts, capacity):
    summed = lax.psum(partial_value, "tensor").astype(jnp.bfloat16)
    arrived = lax.all_to_all(summed, "expert", split_axis=0, concat_axis=0, tiled=True)
    flat_rows = arrived.reshape(experts * capacity, -1)
    return jnp.einsum("te,ed->td", table, flat_rows, preferred_element_type=jnp.float32).astype(
        jnp.bfloat16
    )


def diagonal_sums(matrix):
    heads_here, rows_count, cols_count = matrix.shape
    flipped = matrix[:, ::-1, :]
    padded = jnp.concatenate(
        [flipped, jnp.zeros((heads_here, rows_count, rows_count), matrix.dtype)], 2
    )
    flat = padded.reshape(heads_here, rows_count * (cols_count + rows_count))
    flat = flat[:, : rows_count * (cols_count + rows_count - 1)]
    skewed = flat.reshape(heads_here, rows_count, cols_count + rows_count - 1)
    return jnp.sum(skewed, 1)


def toeplitz_rows(per_offset, rows_count, cols_count):
    heads_here, span = per_offset.shape
    rolled = jnp.concatenate([per_offset[:, rows_count - 1 :], per_offset[:, : rows_count - 1]], 1)
    tiled = jnp.tile(rolled, (1, rows_count))[:, : rows_count * (span - 1)]
    return tiled.reshape(heads_here, rows_count, span - 1)[:, :, :cols_count]


def shards(
    tokens,
    gain_attn,
    w_qkv,
    w_proj,
    rel_bias,
    gain_ffn,
    w_router,
    w_in,
    w_out,
    routes,
    segment_ids,
    cotangent,
):
    length = tokens.shape[0]
    experts = w_router.shape[1]
    capacity = max(2, 3 * length // (2 * experts))
    heads_here = rel_bias.shape[0]
    bucket_count = rel_bias.shape[1]
    inner_here = w_proj.shape[0]
    head_dim = inner_here // heads_here
    scale = head_dim ** (-0.5)
    block = min(512, length)
    blocks = length // block
    segments = segment_ids[0]
    route = routes[:, 0]
    positions = jnp.arange(length, dtype=jnp.int32)
    onehot_low = (route[:, None] == jnp.arange(experts, dtype=jnp.int32)[None, :]).astype(
        jnp.bfloat16
    )
    onehot = onehot_low.astype(jnp.float32)
    lower_ones = (positions[:, None] >= positions[None, :]).astype(jnp.bfloat16)
    running = jnp.dot(lower_ones, onehot_low, preferred_element_type=jnp.float32)
    slot = (jnp.sum(running * onehot, 1) - 1.0).astype(jnp.int32)
    flat_id = route * capacity + slot
    table = (flat_id[:, None] == jnp.arange(experts * capacity, dtype=jnp.int32)[None, :]).astype(
        jnp.bfloat16
    )
    offset_base = jnp.arange(length + block - 1, dtype=jnp.int32) - (block - 1)
    bucket_ids = jnp.arange(bucket_count, dtype=jnp.int32)

    def fold_of(start):
        offset_buckets = bucket_of(offset_base - start)
        return (offset_buckets[:, None] == bucket_ids[None, :]).astype(jnp.float32)

    residual = tokens.astype(jnp.float32)
    normed1 = norm_rows(residual, gain_attn).astype(jnp.bfloat16)
    projected = jnp.einsum(
        "sd,tdi->tsi", normed1, w_qkv, preferred_element_type=jnp.float32
    ).astype(jnp.bfloat16)
    queries = projected[0].reshape(length, heads_here, head_dim)
    keys = projected[1].reshape(length, heads_here, head_dim)
    values = projected[2].reshape(length, heads_here, head_dim)

    def scores_of(start, fold_table):
        per_offset = jnp.dot(rel_bias, fold_table.T, precision=HIGH)
        position_bias = toeplitz_rows(per_offset, block, length)
        raw = (
            jnp.einsum(
                "qhd,khd->hqk",
                queries[start : start + block],
                keys,
                preferred_element_type=jnp.float32,
            )
            * scale
        )
        same_doc = segments[start : start + block][:, None] == segments[None, :]
        return jnp.where(same_doc[None], raw + position_bias, -1e30)

    attended_blocks = []
    lse_blocks = []
    for block_id in range(blocks):
        masked = scores_of(block_id * block, fold_of(block_id * block))
        top_score = jnp.max(masked, -1, keepdims=True)
        log_total = jnp.log(jnp.sum(jnp.exp(masked - top_score), -1, keepdims=True)) + top_score
        probs = jnp.exp(masked - log_total)
        lse_blocks.append(log_total)
        attended_blocks.append(
            jnp.einsum(
                "hqk,khd->qhd",
                probs.astype(jnp.bfloat16),
                values,
                preferred_element_type=jnp.float32,
            )
        )
    attended = jnp.concatenate(attended_blocks, 0).reshape(length, inner_here).astype(jnp.bfloat16)
    head_part = jnp.dot(attended, w_proj, preferred_element_type=jnp.float32)
    hidden1 = residual + lax.psum(head_part, "tensor")
    normed2 = norm_rows(hidden1, gain_ffn).astype(jnp.bfloat16)
    logits = jnp.dot(normed2, w_router, preferred_element_type=jnp.float32)
    router_probs = jax.nn.softmax(logits, -1)
    gate = jnp.sum(router_probs * onehot, -1)
    received = send_rows(normed2, table, experts, capacity)
    pre = jnp.einsum("sxcd,xdf->sxcf", received, w_in, preferred_element_type=jnp.float32)
    act = jax.nn.gelu(pre).astype(jnp.bfloat16)
    expert_part = jnp.einsum("sxcf,xfd->sxcd", act, w_out, preferred_element_type=jnp.float32)
    returned = take_back(expert_part, table, experts, capacity).astype(jnp.float32)
    output = (hidden1 + gate[:, None] * returned).astype(jnp.bfloat16)
    grad_out = cotangent.astype(jnp.float32)
    gate_grad = jnp.sum(grad_out * returned, -1)
    routed = (gate[:, None] * grad_out).astype(jnp.bfloat16)
    grad_received = send_rows(routed, table, experts, capacity)
    grad_act = jnp.einsum(
        "sxcd,xfd->sxcf", grad_received, w_out, preferred_element_type=jnp.float32
    )
    unused_act, gelu_pull = jax.vjp(jax.nn.gelu, pre)
    grad_pre = gelu_pull(grad_act)[0].astype(jnp.bfloat16)
    grad_w_out = jnp.einsum(
        "sxcf,sxcd->xfd", act, grad_received, preferred_element_type=jnp.float32
    )
    grad_w_in = jnp.einsum("sxcd,sxcf->xdf", received, grad_pre, preferred_element_type=jnp.float32)
    input_part = jnp.einsum("sxcf,xdf->sxcd", grad_pre, w_in, preferred_element_type=jnp.float32)
    routed_grad = take_back(input_part, table, experts, capacity).astype(jnp.float32)
    prob_grad = onehot * gate_grad[:, None]
    logit_grad = router_probs * (prob_grad - jnp.sum(prob_grad * router_probs, -1, keepdims=True))
    grad_router = jnp.dot(normed2.astype(jnp.float32).T, logit_grad, precision=HIGH)
    grad_normed2 = routed_grad + jnp.dot(logit_grad, w_router.astype(jnp.float32).T, precision=HIGH)
    unused_norm, norm_pull = jax.vjp(norm_rows, hidden1, gain_ffn)
    back_hidden, grad_gain_ffn = norm_pull(grad_normed2)
    grad_hidden1 = grad_out + back_hidden
    out_grad = grad_hidden1.astype(jnp.bfloat16)
    grad_proj = jnp.einsum("si,sd->id", attended, out_grad, preferred_element_type=jnp.float32)
    attended_grad = jnp.einsum(
        "sd,id->si", out_grad, w_proj, preferred_element_type=jnp.float32
    ).astype(jnp.bfloat16)
    attended_grad = attended_grad.reshape(length, heads_here, head_dim)
    key_grad = jnp.zeros((length, heads_here, head_dim), jnp.float32)
    value_grad = jnp.zeros((length, heads_here, head_dim), jnp.float32)
    grad_rel = jnp.zeros((heads_here, bucket_count), jnp.float32)
    query_grads = []
    for block_id in range(blocks):
        start = block_id * block
        fold_table = fold_of(start)
        masked = scores_of(start, fold_table)
        probs = jnp.exp(masked - lse_blocks[block_id])
        grad_rows = attended_grad[start : start + block]
        prob_part = jnp.einsum(
            "qhd,khd->hqk", grad_rows, values, preferred_element_type=jnp.float32
        )
        row_delta = jnp.sum(probs * prob_part, -1, keepdims=True)
        score_grad = (probs * (prob_part - row_delta)).astype(jnp.bfloat16)
        query_grads.append(
            (
                jnp.einsum("hqk,khd->qhd", score_grad, keys, preferred_element_type=jnp.float32)
                * scale
            ).astype(jnp.bfloat16)
        )
        key_grad = (
            key_grad
            + jnp.einsum(
                "hqk,qhd->khd",
                score_grad,
                queries[start : start + block],
                preferred_element_type=jnp.float32,
            )
            * scale
        )
        value_grad = value_grad + jnp.einsum(
            "hqk,qhd->khd",
            probs.astype(jnp.bfloat16),
            grad_rows,
            preferred_element_type=jnp.float32,
        )
        per_offset = diagonal_sums(score_grad.astype(jnp.float32))
        grad_rel = grad_rel + jnp.dot(per_offset, fold_table, precision=HIGH)
    stacked_grad = jnp.stack(
        [
            jnp.concatenate(query_grads, 0).reshape(length, inner_here),
            key_grad.astype(jnp.bfloat16).reshape(length, inner_here),
            value_grad.astype(jnp.bfloat16).reshape(length, inner_here),
        ]
    )
    grad_qkv = jnp.einsum("sd,tsi->tdi", normed1, stacked_grad, preferred_element_type=jnp.float32)
    normed1_part = jnp.einsum(
        "tsi,tdi->sd", stacked_grad, w_qkv, preferred_element_type=jnp.float32
    )
    grad_normed1 = lax.psum(normed1_part.astype(jnp.bfloat16), "tensor").astype(jnp.float32)
    unused_first, first_pull = jax.vjp(norm_rows, residual, gain_attn)
    back_input, grad_gain_attn = first_pull(grad_normed1)
    grad_input = grad_hidden1 + back_input
    grad_gain_attn, grad_qkv, grad_proj, grad_rel, grad_gain_ffn, grad_router = lax.psum(
        (grad_gain_attn, grad_qkv, grad_proj, grad_rel, grad_gain_ffn, grad_router), "expert"
    )
    return (
        output,
        grad_input,
        grad_gain_attn,
        grad_qkv,
        grad_proj,
        grad_rel,
        grad_gain_ffn,
        grad_router,
        grad_w_in,
        grad_w_out,
    )


def solution(mesh):
    placed = (
        P("expert", None),
        P(),
        P(None, None, "tensor"),
        P("tensor", None),
        P("tensor", None),
        P(),
        P(),
        P("expert", None, "tensor"),
        P("expert", "tensor", None),
        P("expert", None),
        P("expert", None),
        P("expert", None),
    )
    return jax.shard_map(
        shards,
        mesh=mesh,
        in_specs=placed,
        out_specs=(
            P("expert", None),
            P("expert", None),
            P(),
            P(None, None, "tensor"),
            P("tensor", None),
            P("tensor", None),
            P(),
            P(),
            P("expert", None, "tensor"),
            P("expert", "tensor", None),
        ),
        check_vma=False,
    )
```

profile of v0, /device:TPU:0, one launch (start us, length us, event | category | flops | bytes accessed | tf_op | source)
XLA Modules:
  0.0 1002.5 jit_solution(10632361152032956232)
XLA Ops:
  11.9 2.9 fusion.102
  16.6 4.8 tile.10
  21.4 15.3 %reshape.325 = f32[2357760]{0:T(1024)} reshape(f32[3,512,1535]{2,1,0:T(8,128)} %tile.10) | data formatting | bytes 18862080
  36.7 13.1 %tile.11 = f32[3,785920]{1,0:T(4,128)} reshape(f32[2357760]{0:T(1024)} %reshape.325) | data formatting | bytes 18862080 | tf_op jit(solution)/shard_map/tile | solution.py:57
  49.8 11.2 %slice.117 = f32[3,785408]{1,0:T(4,128)} slice(f32[3,785920]{1,0:T(4,128)} %tile.11), slice={[0:3], [0:785408]} | slice | bytes 18849792 | tf_op jit(solution)/shard_map/slice | solution.py:57
  61.0 13.2 %reshape.327 = f32[2356224]{0:T(1024)} reshape(f32[3,785408]{1,0:T(4,128)} %slice.117) | data formatting | bytes 18849792
  74.2 11.0 %reshape.302 = f32[3,512,1534]{2,1,0:T(8,128)} reshape(f32[2356224]{0:T(1024)} %reshape.327) | data formatting | bytes 18849792 | tf_op jit(solution)/shard_map/reshape | solution.py:58
  86.6 4.5 fusion.163
  93.8 4.8 tile.8
  98.6 15.5 %reshape.329 = f32[2357760]{0:T(1024)} reshape(f32[3,512,1535]{2,1,0:T(8,128)} %tile.8) | data formatting | bytes 18862080
  114.2 13.1 %tile.9 = f32[3,785920]{1,0:T(4,128)} reshape(f32[2357760]{0:T(1024)} %reshape.329) | data formatting | bytes 18862080 | tf_op jit(solution)/shard_map/tile | solution.py:57
  127.3 11.1 %slice.112 = f32[3,785408]{1,0:T(4,128)} slice(f32[3,785920]{1,0:T(4,128)} %tile.9), slice={[0:3], [0:785408]} | slice | bytes 18849792 | tf_op jit(solution)/shard_map/slice | solution.py:57
  138.4 13.2 %reshape.331 = f32[2356224]{0:T(1024)} reshape(f32[3,785408]{1,0:T(4,128)} %slice.112) | data formatting | bytes 18849792
  151.6 11.3 %reshape.301 = f32[3,512,1534]{2,1,0:T(8,128)} reshape(f32[2356224]{0:T(1024)} %reshape.331) | data formatting | bytes 18849792 | tf_op jit(solution)/shard_map/reshape | solution.py:58
  163.0 4.9 fusion.164
  171.9 2.3 fusion.166
  174.8 70.7 %all-reduce.10.cloned.1.call-done = f32[1024,768]{1,0:T(8,128)} async-done(((f32[1024,768]{1,0:T(8,128)}), f32[1024,768]{1,0:T(8,128)}) %all-reduce.10.cloned.1.call-update) | async-done | bytes 3145744 | tf_op jit(solution)/shard_map/psum | solution.py:148
  245.5 2.4 multiply_reduce_fusion.4
  248.3 3.8 fusion.22
  252.1 59.6 %all_to_all.20 = bf16[8,1,192,768]{3,2,1,0:T(8,128)(2,1)S(1)} all-to-all(bf16[8,1,192,768]{3,2,1,0:T(8,128)(2,1)S(1)} %bitcast.227), channel_id=1, replica_groups=mesh['expert'=8,'tensor'=4] {'expert'}, dimensions={0} | all-to-all | bytes 4718592 | tf_op jit(solution)/shard_map/all_to_all | solution.py:30
  313.1 2.1 fusion.48
  315.2 2.2 copy-done.44
  317.4 5.1 fusion.50
  322.5 84.9 %all-reduce.15 = bf16[8,1,192,768]{3,2,0,1:T(8,128)(2,1)} all-reduce(f32[8,1,192,768]{3,2,0,1:T(8,128)} %fusion.50), channel_id=1, replica_groups=mesh['expert'=8,'tensor'=4] {'tensor'}, use_global_device_ids=true, to_apply=%region_11.12 | all-reduce | flops 1179648 | bytes 7077888 | tf_op jit(solution)/shard_map/psum | solution.py:34
  407.5 4.5 all-to-all-start.1
  412.0 1.9 fusion.165
  414.0 53.0 %all-to-all-done.1 = bf16[8,1,192,768]{3,2,1,0:T(8,128)(2,1)} async-done(((bf16[8,1,192,768]{3,2,1,0:T(8,128)(2,1)}), bf16[8,1,192,768]{3,2,1,0:T(8,128)(2,1)}, u32[]{:S(2)}, u32[]{:S(2)}) %all-to-all-start.1) | async-done | bytes 2359328 | tf_op jit(solution)/shard_map/all_to_all | solution.py:35
  466.9 6.2 fusion.29
  473.2 3.5 fusion.23
  476.7 57.6 %all_to_all.21 = bf16[8,1,192,768]{3,2,1,0:T(8,128)(2,1)S(1)} all-to-all(bf16[8,1,192,768]{3,2,1,0:T(8,128)(2,1)S(1)} %bitcast.228), channel_id=1, replica_groups=mesh['expert'=8,'tensor'=4] {'expert'}, dimensions={0} | all-to-all | bytes 4718592 | tf_op jit(solution)/shard_map/all_to_all | solution.py:30
  534.3 4.3 fusion.14
  540.1 4.2 fusion.53
  544.3 85.3 %all-reduce.16 = bf16[8,1,192,768]{3,2,0,1:T(8,128)(2,1)} all-reduce(f32[8,1,192,768]{3,2,0,1:T(8,128)} %fusion.53), channel_id=1, replica_groups=mesh['expert'=8,'tensor'=4] {'tensor'}, use_global_device_ids=true, to_apply=%region_12.13 | all-reduce | flops 1179648 | bytes 7077888 | tf_op jit(solution)/shard_map/psum | solution.py:34
  629.6 4.4 all-to-all-start.3
  634.0 2.7 fusion.115
  636.8 7.0 fusion.56
  643.8 44.9 %all-to-all-done.3 = bf16[8,1,192,768]{3,2,1,0:T(8,128)(2,1)} async-done(((bf16[8,1,192,768]{3,2,1,0:T(8,128)(2,1)}), bf16[8,1,192,768]{3,2,1,0:T(8,128)(2,1)}, u32[]{:S(2)}, u32[]{:S(2)}) %all-to-all-start.3) | async-done | bytes 2359328 | tf_op jit(solution)/shard_map/all_to_all | solution.py:35
  688.7 4.7 fusion.67
  693.4 2.4 multiply_reduce_fusion.2
  695.9 2.5 convert_add_fusion.1
  700.6 1.9 multiply_reduce_fusion.1
  707.3 1.9 multiply_reduce_fusion
  714.1 2.6 bitcast_convert_fusion
  716.8 5.8 fusion.61
  722.6 46.3 %rev.7 = f32[3,512,1024]{2,1,0:T(8,128)} reverse(bf16[3,512,1024]{2,1,0:T(8,128)(2,1)} %copy-done.4), dimensions={1} | reverse | bytes 9437184 | tf_op jit(solution)/shard_map/rev | solution.py:44
  769.0 45.8 %rev.6 = f32[3,512,1024]{2,1,0:T(8,128)} reverse(bf16[3,512,1024]{2,1,0:T(8,128)(2,1)} %copy-done.8), dimensions={1} | reverse | bytes 9437184 | tf_op jit(solution)/shard_map/rev | solution.py:44
  814.8 3.2 fusion.95
  818.0 2.4 fusion.72
  820.5 4.0 pad_bitcast_fusion
  824.5 19.9 %copy.30 = f32[1,3,512,1536]{3,1,2,0:T(4,128)S(1)} copy(f32[1,3,512,1536]{3,2,1,0:T(8,128)S(1)} %pad_bitcast_fusion) | data formatting | bytes 18874368
  844.4 5.8 slice.122
  850.1 13.3 %reshape.335 = f32[2357760]{0:T(1024)} reshape(f32[3,785920]{1,0:T(4,128)} %slice.122) | data formatting | bytes 18862080
  863.5 15.7 %reshape.316 = f32[3,512,1535]{2,1,0:T(8,128)} reshape(f32[2357760]{0:T(1024)} %reshape.335) | data formatting | bytes 18862080 | tf_op jit(solution)/shard_map/reshape | solution.py:50
  879.2 4.1 pad_bitcast_fusion.1
  883.4 19.9 %copy.29 = f32[1,3,512,1536]{3,1,2,0:T(4,128)S(1)} copy(f32[1,3,512,1536]{3,2,1,0:T(8,128)S(1)} %pad_bitcast_fusion.1) | data formatting | bytes 18874368
  903.2 6.0 slice.121
  909.2 13.3 %reshape.333 = f32[2357760]{0:T(1024)} reshape(f32[3,785920]{1,0:T(4,128)} %slice.121) | data formatting | bytes 18862080
  922.5 15.9 %reshape.314 = f32[3,512,1535]{2,1,0:T(8,128)} reshape(f32[2357760]{0:T(1024)} %reshape.333) | data formatting | bytes 18862080 | tf_op jit(solution)/shard_map/reshape | solution.py:50
  938.4 4.2 reduce_sum.192
  942.6 4.2 reduce_sum.191
  947.9 2.9 fusion.27
  950.8 36.2 %all-reduce.2 = (f32[768]{0:T(1024)}, f32[3,32]{1,0:T(4,128)}, f32[768]{0:T(1024)}, f32[768,8]{0,1:T(8,128)}) all-reduce(f32[768]{0:T(1024)S(1)} %get-tuple-element.12, f32[3,32]{1,0:T(4,128)S(1)} %convolution_add_fusion.2, f32[768]{0:T(1024)S(1)} %get-tuple-element.10, ...), channel_id=1, replica_groups=mesh['expert'=8,'tensor'=4] {'expert'}, use_global_device_ids=true, to_apply=%region_21.22 | all-reduce | flops 7776 | bytes 62208 | tf_op jit(solution)/shard_map/psum | solution.py:241
  987.0 5.0 fusion.30
  992.0 2.9 copy.39
  (166 shorter events, 31.6 us)
Async XLA Ops:
  7.2 310.2 %copy-start = (bf16[1,768,768]{2,1,0:T(8,128)(2,1)S(1)}, bf16[1,768,768]{2,1,0:T(8,128)(2,1)}, u32[]{:S(2)}) copy-start(bf16[1,768,768]{2,1,0:T(8,128)(2,1)} %param.20) | copy-start | bytes 3538948
  7.2 238.3 %all-reduce.10.cloned.1.call-start = ((), (), s32[]{:S(2)}) async-start(), calls=%async_computation.4 | async-start | bytes 6291456 | tf_op jit(solution)/shard_map/psum | solution.py:148
  7.3 7.5 copy-start.37
  7.3 2.7 copy-start.39
  8.6 6.1 copy-start.33
  10.0 4.8 copy-start.34
  11.9 2.9 copy-start.30
  11.9 2.9 copy-start.28
  14.8 1.7 copy-start.36
  14.8 1.7 slice-start.7
  16.5 70.1 %copy-start.11 = (bf16[1,1024,192]{1,2,0:T(8,128)(2,1)}, bf16[1,1024,192]{1,2,0:T(8,128)(2,1)S(1)}, u32[]{:S(2)}) copy-start(bf16[1,1024,192]{1,2,0:T(8,128)(2,1)S(1)} %get-tuple-element.28) | copy-start | bytes 1179652
  91.1 2.6 copy-start.2
  91.1 2.6 slice-start.6
  151.6 17.8 %slice-start = ((s8[6291456]{0:T(1024)(128)(4,1)}), s8[2097152]{0:T(1024)(128)(4,1)S(1)}, s32[]{:S(2)}) async-start(s8[6291456]{0:T(1024)(128)(4,1)} %bitcast.206), calls=%async_computation.7 | async-start | bytes 4194304
  163.0 6.4 slice-start.1
  167.9 2.7 copy-start.3
  167.9 1.5 copy-start.13
  170.6 1.2 copy-start.22
  171.9 2.3 copy-start.26
  171.9 73.6 %copy-start.9 = (bf16[1024,768]{1,0:T(8,128)(2,1)S(1)}, bf16[1024,768]{1,0:T(8,128)(2,1)}, u32[]{:S(2)}) copy-start(bf16[1024,768]{1,0:T(8,128)(2,1)} %param.12) | copy-start | bytes 4718596
  174.7 73.2 %copy-start.32 = (f32[768]{0:T(1024)S(1)}, f32[768]{0:T(1024)}, u32[]{:S(2)}) copy-start(f32[768]{0:T(1024)} %param.17) | copy-start | bytes 9220
  247.9 4.2 copy-start.5
  248.2 3.8 copy-start.10
  252.1 61.0 %copy-start.41 = (bf16[1,768,768]{2,1,0:T(8,128)(2,1)S(1)}, bf16[1,768,768]{2,1,0:T(8,128)(2,1)}, u32[]{:S(2)}) copy-start(bf16[1,768,768]{2,1,0:T(8,128)(2,1)} %param.19) | copy-start | bytes 3538948
  311.7 1.4 copy-start.15
  315.2 2.2 copy-start.44
  407.5 4.5 copy-start.27
  407.5 59.5 %all-to-all-start.1 = ((bf16[8,1,192,768]{3,2,1,0:T(8,128)(2,1)}), bf16[8,1,192,768]{3,2,1,0:T(8,128)(2,1)}, u32[]{:S(2)}, u32[]{:S(2)}) async-start(bf16[8,1,192,768]{3,2,1,0:T(8,128)(2,1)} %bitcast.223), calls=%async_computation.1 | async-start | bytes 4718592 | tf_op jit(solution)/shard_map/all_to_all | solution.py:35
  466.9 6.2 copy-start.19
  466.9 67.3 %slice-start.8 = ((s8[4718592]{0:T(1024)(128)(4,1)}), s8[4194304]{0:T(1024)(128)(4,1)S(1)}, s32[]{:S(2)}) async-start(s8[4718592]{0:T(1024)(128)(4,1)} %bitcast.256), calls=%async_computation.15 | async-start | bytes 8388608
  473.1 61.1 %slice-start.9 = ((s8[4718592]{0:T(1024)(128)(4,1)}), s8[524288]{0:T(1024)(128)(4,1)S(1)}, s32[]{:S(2)}) async-start(s8[4718592]{0:T(1024)(128)(4,1)} %bitcast.256), calls=%async_computation.16 | async-start | bytes 1048576
  534.3 4.4 copy-start.17
  534.3 5.8 copy-start.42
  538.7 1.4 copy-start.16
  629.6 59.1 %all-to-all-start.3 = ((bf16[8,1,192,768]{3,2,1,0:T(8,128)(2,1)}), bf16[8,1,192,768]{3,2,1,0:T(8,128)(2,1)}, u32[]{:S(2)}, u32[]{:S(2)}) async-start(bf16[8,1,192,768]{3,2,1,0:T(8,128)(2,1)} %bitcast.222), calls=%async_computation.3 | async-start | bytes 4718592 | tf_op jit(solution)/shard_map/all_to_all | solution.py:35
  634.0 313.9 %all-reduce.12.cloned.1.call-start = ((), (), s32[]{:S(2)}) async-start(), calls=%async_computation.5 | async-start | bytes 3145728 | tf_op jit(solution)/shard_map/psum | solution.py:237
  688.7 4.7 copy-start.6
  693.4 2.5 copy-start.20
  693.4 2.5 copy-start.21
  695.9 3.3 slice-start.4
  695.9 2.5 copy-start.23
  695.9 3.5 slice-start.5
  698.4 2.2 copy-start.7
  699.4 1.2 copy-start.14
  702.5 4.7 slice-start.2
  702.5 1.4 copy-start.12
  702.5 4.7 slice-start.3
  703.9 3.3 copy-start.8
  704.0 2.6 copy-start.18
  711.8 1.8 copy-start.4
  712.9 1.2 copy-start.43
  716.7 275.3 %all-reduce.14.cloned.1.call-start = ((), (), s32[]{:S(2)}) async-start(), calls=%async_computation.6 | async-start | bytes 4718592 | tf_op jit(solution)/shard_map/psum | solution.py:241
  814.8 3.2 copy-start.29
  814.8 3.2 copy-start.35
  942.6 4.3 copy-start.40
  942.6 4.8 copy-start.38
  946.9 3.9 copy-start.25
  946.9 40.1 %copy-start.31 = (f32[1024]{0:T(1024)S(1)}, f32[1024]{0:T(1024)}, u32[]{:S(2)}) copy-start(f32[1024]{0:T(1024)} %copy-done.30) | copy-start | bytes 12292
  987.0 8.7 copy-start.1
  992.0 2.9 copy-start.24
Sparse Core Ops, SparseCore 0:
  174.3 71.1 all-reduce.9
  716.8 40.9 all-reduce.11
  820.6 107.1 all-reduce.13
where the time goes:
time: 1020 us; the launch traced here: 1000 us
  local copies, waits for them, and re-layouts  362 us (35%)
  blocking collectives  324 us (32%)
  waiting for transfers between devices  169 us (17%)
  matrix products  93.4 us (9%)
  other arithmetic  30.9 us (3%)
  between operations  15 us (1%)
    psum x2, blocking collectives, take_back(): summed = lax.psum(partial_value, 'tensor').astype(jnp.bfloat16)  170 us
    unnamed x118, local copies, waits for them, and re-layouts  144 us
    all_to_all x2, blocking collectives, send_rows(): lax.all_to_all(outgoing, 'expert', split_axis=0, concat_axis=0, tiled=True)  117 us
    all_to_all x2, waiting for transfers between devices, take_back(): lax.all_to_all(summed, 'expert', split_axis=0, concat_axis=0, tiled=True)  97.9 us
    rev x2, local copies, waits for them, and re-layouts, diagonal_sums(): flipped = matrix[:, ::-1, :]  92.2 us
    psum x1, waiting for transfers between devices, shards(): hidden1 = residual + lax.psum(head_part, 'tensor')  70.7 us
    psum x1, blocking collectives, shards(): lax.psum((grad_gain_attn, grad_qkv, grad_proj, grad_rel, grad_gain_ffn, g...  36.2 us
    another operation x4, local copies, waits for them, and re-layouts, toeplitz_rows(): tiled = jnp.tile(rolled, (1, rows_count))[:, :rows_count * (span - 1)]  36 us
  transfers between devices with their start and end apart: 5, of which 3 were waited for; matrix products, arithmetic and copies ran while one was open for 25% of the time, Pallas kernels for 0%

commit v1 on v0

v1 whole, which is shorter than its diff:
```python
import functools

import jax
import jax.numpy as jnp
from jax import lax
from jax.experimental import pallas as pl
from jax.experimental.pallas import tpu as pltpu
from jax.sharding import PartitionSpec as P

FAR_LIMITS = (12, 16, 23, 32, 46, 64, 91)
HIGH = lax.Precision.HIGHEST
F32 = jnp.float32
BF16 = jnp.bfloat16
MASKED = -1e30
QB = 256
PAD = 256
FAR = FAR_LIMITS[-1]

STEPS = (
    [(1 - limit, 14 - i) for i, limit in enumerate(reversed(FAR_LIMITS))]
    + [(-n, n) for n in range(7, -1, -1)]
    + [(n, 16 + n) for n in range(1, 8)]
    + [(8, 24)]
    + [(limit, 25 + i) for i, limit in enumerate(FAR_LIMITS)]
)


def norm_rows(values, gain):
    return values * lax.rsqrt(jnp.mean(values * values, -1, keepdims=True) + 1e-06) * gain


def nt_dot(left, right):
    return lax.dot_general(left, right, (((1,), (1,)), ((), ())), preferred_element_type=F32)


def nn_dot(left, right):
    return jnp.dot(left, right, preferred_element_type=F32)


def strip_shape(length):
    return 2 * length - QB


def near_rows(length):
    base = length - QB
    first = (base - FAR) // 32 * 32
    last = -(-(base + 127 + FAR) // 32) * 32
    return base, first, last


def build_strip(strip_ref, bias_ref, length, heads):
    total = strip_shape(length)
    base, first, last = near_rows(length)
    for h in range(heads):
        low = jnp.full((8, 128), bias_ref[h, 15], F32)
        high = jnp.full((8, 128), bias_ref[h, 31], F32)
        for half in range(QB // 128):
            cols = slice(half * 128, half * 128 + 128)
            lo_end, hi_start = first + half * 128, last + half * 128
            strip_ref[h, 0:lo_end, cols] = jnp.broadcast_to(low[:1], (lo_end, 128))
            strip_ref[h, hi_start:total, cols] = jnp.broadcast_to(high[:1], (total - hi_start, 128))
    for start in range(first, last, 32):
        offset = (
            lax.broadcasted_iota(jnp.int32, (32, 128), 0)
            - lax.broadcasted_iota(jnp.int32, (32, 128), 1)
            + (start - base)
        )
        tiles = [jnp.full((32, 128), bias_ref[h, 15], F32) for h in range(heads)]
        for begin, bucket in STEPS:
            reached = offset >= begin
            tiles = [jnp.where(reached, bias_ref[h, bucket], tiles[h]) for h in range(heads)]
        for h in range(heads):
            for half in range(QB // 128):
                at = start + half * 128
                strip_ref[h, at : at + 32, half * 128 : half * 128 + 128] = tiles[h]


def head_lanes(rows, h, dim, keep_tail, heads):
    lane = lax.broadcasted_iota(jnp.int32, (rows, PAD), 1)
    inside = (lane >= h * dim) & (lane < (h + 1) * dim)
    if keep_tail:
        inside = inside | (lane >= heads * dim)
    return inside


def attend_kernel(length, heads, dim, proj_ref, vt_ref, bias_ref, att_ref, lse_ref, kh_ref, strip_ref):
    build_strip(strip_ref, bias_ref, length, heads)
    keys = proj_ref[:, PAD : 2 * PAD]
    for h in range(heads):
        kh_ref[h] = jnp.where(head_lanes(length, h, dim, True, heads), keys, jnp.zeros_like(keys))

    def block(b, carry):
        at = pl.multiple_of(b * QB, QB)
        from_row = pl.multiple_of(length - QB - b * QB, QB)
        queries = proj_ref[pl.ds(at, QB), 0:PAD]
        for h in range(heads):
            scores = nt_dot(kh_ref[h], queries) + strip_ref[h, pl.ds(from_row, length), :]
            top = jnp.max(scores, 0, keepdims=True)
            probs = jnp.exp(scores - top)
            total = jnp.sum(probs, 0, keepdims=True)
            out = nn_dot(vt_ref[h * dim : (h + 1) * dim, :], probs.astype(BF16))
            att_ref[h * dim : (h + 1) * dim, pl.ds(at, QB)] = (out / total).astype(BF16)
            lse_ref[h : h + 1, pl.ds(at, QB)] = top + jnp.log(total)
        return carry

    lax.fori_loop(0, length // QB, block, 0)


def attend_back_kernel(
    length, heads, dim,
    proj_ref, kt_ref, lse_ref, da_ref, bias_ref,
    dqkv_ref, drel_ref,
    kh_ref, vh_ref, strip_ref, dstrip_ref, pcat_ref, dcat_ref, dacat_ref, qcat_ref, dk_ref, dv_ref, dqt_ref,
):
    inner = heads * dim
    scale = dim ** (-0.5)
    total = strip_shape(length)
    base, first, last = near_rows(length)
    build_strip(strip_ref, bias_ref, length, heads)
    dstrip_ref[...] = jnp.zeros_like(dstrip_ref)
    dk_ref[...] = jnp.zeros_like(dk_ref)
    dv_ref[...] = jnp.zeros_like(dv_ref)
    dqt_ref[...] = jnp.zeros_like(dqt_ref)
    keys = proj_ref[:, PAD : 2 * PAD]
    values = proj_ref[:, 2 * PAD : 3 * PAD]
    for h in range(heads):
        kh_ref[h] = jnp.where(head_lanes(length, h, dim, True, heads), keys, jnp.zeros_like(keys))
        vh_ref[h] = jnp.where(head_lanes(length, h, dim, False, heads), values, jnp.zeros_like(values))

    def block(b, carry):
        at = pl.multiple_of(b * QB, QB)
        from_row = pl.multiple_of(length - QB - b * QB, QB)
        queries = proj_ref[pl.ds(at, QB), 0:PAD]
        grads = da_ref[pl.ds(at, QB), :]
        for h in range(heads):
            mine = head_lanes(QB, h, dim, False, heads)
            cols = slice(h * QB, (h + 1) * QB)
            qcat_ref[cols, :] = jnp.where(mine, queries, jnp.zeros_like(queries))
            dacat_ref[cols, :] = jnp.where(mine, grads, jnp.zeros_like(grads))
            scores = nt_dot(kh_ref[h], queries) + strip_ref[h, pl.ds(from_row, length), :]
            probs = jnp.exp(scores - lse_ref[h : h + 1, pl.ds(at, QB)])
            weighted = probs * nt_dot(vh_ref[h], grads)
            delta = jnp.sum(weighted, 0, keepdims=True)
            dscore = weighted - probs * delta
            dstrip_ref[h, pl.ds(from_row, length), :] += dscore
            dlow = dscore.astype(BF16)
            pcat_ref[:, cols] = probs.astype(BF16)
            dcat_ref[:, cols] = dlow
            dqt_ref[h * dim : (h + 1) * dim, :] = nn_dot(kt_ref[h * dim : (h + 1) * dim, :], dlow) * scale
        dk_ref[...] += nn_dot(dcat_ref[...], qcat_ref[...])
        dv_ref[...] += nn_dot(pcat_ref[...], dacat_ref[...])
        dqkv_ref[0, pl.ds(at, QB), :] = dqt_ref[...].T[:, :inner].astype(BF16)
        return carry

    lax.fori_loop(0, length // QB, block, 0)
    dqkv_ref[1] = dk_ref[:, :inner].astype(BF16)
    dqkv_ref[2] = dv_ref[:, :inner].astype(BF16)

    offset = (
        lax.broadcasted_iota(jnp.int32, (last - first, 128), 0)
        - lax.broadcasted_iota(jnp.int32, (last - first, 128), 1)
        + (first - base)
    )
    begins = [-(1 << 20)] + [begin for begin, bucket in STEPS] + [1 << 20]
    buckets = [15] + [bucket for begin, bucket in STEPS]
    for h in range(heads):
        near = jnp.zeros((last - first, 128), F32)
        low = jnp.zeros((1, 128), F32)
        high = jnp.zeros((1, 128), F32)
        for half in range(QB // 128):
            cols = slice(half * 128, half * 128 + 128)
            lo_end, hi_start = first + half * 128, last + half * 128
            near = near + dstrip_ref[h, lo_end:hi_start, cols]
            low = low + jnp.sum(dstrip_ref[h, 0:lo_end, cols], 0, keepdims=True)
            high = high + jnp.sum(dstrip_ref[h, hi_start:total, cols], 0, keepdims=True)
        drel_ref[h, 16:17, :] = jnp.zeros((1, 128), F32)
        for i, bucket in enumerate(buckets):
            inside = (offset >= begins[i]) & (offset < begins[i + 1])
            row = jnp.sum(jnp.where(inside, near, 0.0), 0, keepdims=True)
            if bucket == 15:
                row = row + low
            if bucket == 31:
                row = row + high
            drel_ref[h, bucket : bucket + 1, :] = row


def whole_vmem(count):
    return [pl.BlockSpec(memory_space=pltpu.VMEM)] * count


def attend(proj, vt, rel_bias, dim):
    length = proj.shape[0]
    heads = rel_bias.shape[0]
    return pl.pallas_call(
        functools.partial(attend_kernel, length, heads, dim),
        out_shape=(
            jax.ShapeDtypeStruct((heads * dim, length), BF16),
            jax.ShapeDtypeStruct((8, length), F32),
        ),
        in_specs=whole_vmem(2) + [pl.BlockSpec(memory_space=pltpu.SMEM)],
        out_specs=tuple(whole_vmem(2)),
        scratch_shapes=[
            pltpu.VMEM((heads, length, PAD), BF16),
            pltpu.VMEM((heads, strip_shape(length), QB), F32),
        ],
        compiler_params=pltpu.CompilerParams(vmem_limit_bytes=40 << 20),
        cost_estimate=pl.CostEstimate(
            flops=4 * heads * length * length * dim,
            bytes_accessed=4 << 20,
            transcendentals=heads * length * length,
        ),
    )(proj, vt, rel_bias)


def attend_back(proj, kt, lse, da, rel_bias, dim):
    length = proj.shape[0]
    heads, buckets = rel_bias.shape
    return pl.pallas_call(
        functools.partial(attend_back_kernel, length, heads, dim),
        out_shape=(
            jax.ShapeDtypeStruct((3, length, heads * dim), BF16),
            jax.ShapeDtypeStruct((heads, buckets, 128), F32),
        ),
        in_specs=whole_vmem(4) + [pl.BlockSpec(memory_space=pltpu.SMEM)],
        out_specs=tuple(whole_vmem(2)),
        scratch_shapes=[
            pltpu.VMEM((heads, length, PAD), BF16),
            pltpu.VMEM((heads, length, PAD), BF16),
            pltpu.VMEM((heads, strip_shape(length), QB), F32),
            pltpu.VMEM((heads, strip_shape(length), QB), F32),
            pltpu.VMEM((length, heads * QB), BF16),
            pltpu.VMEM((length, heads * QB), BF16),
            pltpu.VMEM((heads * QB, PAD), BF16),
            pltpu.VMEM((heads * QB, PAD), BF16),
            pltpu.VMEM((length, PAD), F32),
            pltpu.VMEM((length, PAD), F32),
            pltpu.VMEM((PAD, QB), F32),
        ],
        compiler_params=pltpu.CompilerParams(vmem_limit_bytes=56 << 20),
        cost_estimate=pl.CostEstimate(
            flops=10 * heads * length * length * dim,
            bytes_accessed=6 << 20,
            transcendentals=heads * length * length,
        ),
    )(proj, kt, lse, da, rel_bias)


def shards(
    tokens,
    gain_attn,
    w_qkv,
    w_proj,
    rel_bias,
    gain_ffn,
    w_router,
    w_in,
    w_out,
    routes,
    segment_ids,
    cotangent,
):
    length, width = tokens.shape
    experts = w_router.shape[1]
    here = w_in.shape[0]
    capacity = max(2, 3 * length // (2 * experts))
    heads_here = rel_bias.shape[0]
    inner_here = w_proj.shape[0]
    head_dim = inner_here // heads_here
    scale = head_dim ** (-0.5)
    members = lax.axis_size("tensor")
    groups = lax.axis_size("expert")
    member = lax.axis_index("tensor")
    group = lax.axis_index("expert")
    share = capacity // members
    segments = segment_ids[0]
    route = routes[:, 0]

    def swap(value, bit):
        return lax.ppermute(value, "tensor", [(i, i ^ bit) for i in range(members)])

    bits = [1 << i for i in range(members.bit_length() - 1)]

    def gather_members(value):
        blocks = {0: value}
        for bit in reversed(bits):
            blocks.update({k ^ bit: swap(block, bit) for k, block in blocks.items()})
        return [blocks[k] for k in range(members)]

    def sum_members(parts):
        held = dict(enumerate(parts))
        for bit in bits:
            for k in [k for k in held if k & bit]:
                held[k ^ bit] = held[k ^ bit] + swap(held.pop(k).astype(BF16), bit).astype(F32)
        return held[0]

    paired = groups <= 8

    def owner_of(k):
        return group ^ k if paired else jnp.int32(k)

    def across(value, k):
        return lax.ppermute(value, "expert", [(i, i ^ k) for i in range(groups)])

    def exchange(value):
        if not paired:
            return lax.all_to_all(value, "expert", split_axis=0, concat_axis=0, tiled=True)
        far_first = sorted(range(1, groups), reverse=True)
        blocks = {k: across(value[k], k) for k in far_first}
        blocks[0] = value[0]
        return jnp.stack([blocks[k] for k in range(groups)])

    def gather_groups(value):
        if not paired:
            return lax.all_gather(value, "expert", axis=0)
        far_first = sorted(range(1, groups), reverse=True)
        blocks = {k: across(value, k) for k in far_first}
        blocks[0] = value
        return jnp.stack([blocks[k] for k in range(groups)])

    def in_order(value):
        if not paired:
            return value
        return jnp.stack([lax.dynamic_index_in_dim(value, group ^ k, 0, False) for k in range(groups)])

    def sum_groups(value, extra=None):
        rows, columns = value.shape
        cut = in_order(value.reshape(groups, rows // groups, columns)).astype(BF16)
        mine = jnp.sum(exchange(cut).astype(F32), 0).astype(BF16)
        if extra is not None:
            mine = jnp.concatenate([mine, extra.astype(BF16)], 0)
        every = gather_groups(mine)
        total = in_order(every[:, : rows // groups]).reshape(rows, columns).astype(F32)
        if extra is None:
            return total
        return total, jnp.sum(every[:, rows // groups :].astype(F32), 0)

    expert_ids = jnp.arange(experts, dtype=jnp.int32)
    onehot_low = (route[:, None] == expert_ids[None, :]).astype(BF16)
    onehot = onehot_low.astype(F32)
    positions = jnp.arange(length, dtype=jnp.int32)
    lower_ones = (positions[:, None] >= positions[None, :]).astype(BF16)
    running = nn_dot(lower_ones, onehot_low)
    slot = (jnp.sum(running * onehot, 1) - 1.0).astype(jnp.int32)
    flat_id = route * capacity + slot

    block_experts = jnp.stack([owner_of(k) for k in range(groups)])
    block_experts = (block_experts[:, None] * here + jnp.arange(here, dtype=jnp.int32)).reshape(-1)

    def ids_of(owner):
        slots = owner * share + jnp.arange(share, dtype=jnp.int32)
        return (block_experts[:, None] * capacity + slots[None, :]).reshape(-1)

    send_table = (ids_of(member)[:, None] == flat_id[None, :]).astype(BF16)
    all_ids = jnp.concatenate([ids_of(member ^ k) for k in range(members)])
    back_table = (flat_id[:, None] == all_ids[None, :]).astype(BF16)

    w_proj_all = jnp.concatenate(gather_members(w_proj), 0)

    residual = tokens.astype(F32)
    normed1 = norm_rows(residual, gain_attn).astype(BF16)
    tail = PAD - inner_here
    w_pad = jnp.pad(w_qkv, ((0, 0), (0, 0), (0, tail)))
    w_all = jnp.concatenate([w_pad[0], w_pad[1], w_pad[2]], 1)
    documents = segments[:, None] == jnp.arange(tail, dtype=jnp.int32)[None, :]
    first_lane = jnp.zeros((length, inner_here), F32)
    extra = jnp.concatenate(
        [
            first_lane,
            jnp.where(documents, 0.0, MASKED),
            first_lane,
            documents.astype(F32),
            jnp.zeros((length, PAD), F32),
        ],
        1,
    ).astype(BF16)
    factors = jnp.where(jnp.arange(3 * PAD) < PAD, scale, 1.0).astype(BF16)
    proj = nn_dot(normed1, w_all).astype(BF16) * factors[None, :] + extra
    kvt = jnp.einsum("tdi,sd->tis", w_qkv[1:], normed1, preferred_element_type=F32).astype(BF16)
    def dispatch(rows):
        out = nn_dot(send_table, rows).astype(BF16).reshape(groups, -1, width)
        return exchange(out).reshape(-1, width)

    cot_share = dispatch(cotangent)
    proj, cot_share, w_proj_all = lax.optimization_barrier((proj, cot_share, w_proj_all))
    attended_t, lse = attend(proj, kvt[1], rel_bias, head_dim)

    attended_all = jnp.concatenate(gather_members(attended_t), 0)
    attended_all, cot_share = lax.optimization_barrier((attended_all, cot_share))
    head_out = lax.dot_general(
        attended_all, w_proj_all, (((0,), (0,)), ((), ())), preferred_element_type=F32
    )
    hidden1 = residual + head_out
    normed2 = norm_rows(hidden1, gain_ffn).astype(BF16)
    logits = nn_dot(normed2, w_router)
    router_probs = jax.nn.softmax(logits, -1)
    gate = jnp.sum(router_probs * onehot, -1)
    grad_out = cotangent.astype(F32)

    share_rows = dispatch(normed2)
    cot_rows = jnp.concatenate(gather_members(cot_share), 0)
    share_rows, cot_rows = lax.optimization_barrier((share_rows, cot_rows))
    received = jnp.concatenate(gather_members(share_rows), 0)

    first, second = w_in[0], w_out[0]
    rows_here = received.shape[0] // members

    def cut(value):
        return [value[k * rows_here : (k + 1) * rows_here] for k in range(members)]

    def summed(value):
        return sum_members(cut(value)).astype(BF16)

    def home(value):
        back = exchange(value.reshape(groups, -1, width)).reshape(-1, width)
        return nn_dot(back_table, jnp.concatenate(gather_members(back), 0)).astype(BF16).astype(F32)

    slot_probs = jax.nn.softmax(nn_dot(received, w_router), -1)
    own = (expert_ids == group).astype(F32)[None, :]
    slot_gate = jnp.sum(slot_probs * own, -1, keepdims=True)
    cot_values = cot_rows.astype(F32)
    grad_received = (slot_gate * cot_values).astype(BF16)
    pre = nn_dot(received, first)
    act = jax.nn.gelu(pre).astype(BF16)
    expert_part = nn_dot(act, second)
    slot_gate_grad = jnp.sum(cot_values * expert_part, -1, keepdims=True)
    slot_logit_grad = (slot_probs * (own - slot_gate) * slot_gate_grad).astype(BF16)
    grad_act = nt_dot(grad_received, second)
    unused_act, gelu_pull = jax.vjp(jax.nn.gelu, pre)
    grad_pre = gelu_pull(grad_act)[0].astype(BF16)
    input_part = nt_dot(grad_pre, first) + nt_dot(slot_logit_grad, w_router)
    grad_share = summed(input_part)
    expert_part, grad_share = lax.optimization_barrier((expert_part, grad_share))
    grad_normed2 = home(grad_share)
    reply_share = summed(expert_part)
    returned = home(reply_share)
    grad_w_out = lax.dot_general(
        act, grad_received, (((0,), (0,)), ((), ())), preferred_element_type=F32
    )
    grad_w_in = lax.dot_general(
        received, grad_pre, (((0,), (0,)), ((), ())), preferred_element_type=F32
    )

    output = (hidden1 + gate[:, None] * returned).astype(BF16)
    gate_grad = jnp.sum(grad_out * returned, -1)
    prob_grad = onehot * gate_grad[:, None]
    logit_grad = router_probs * (prob_grad - jnp.sum(prob_grad * router_probs, -1, keepdims=True))
    grad_router = jnp.dot(normed2.astype(F32).T, logit_grad, precision=HIGH)
    unused_norm, norm_pull = jax.vjp(norm_rows, hidden1, gain_ffn)
    back_hidden, grad_gain_ffn = norm_pull(grad_normed2)
    grad_hidden1 = grad_out + back_hidden
    out_grad = grad_hidden1.astype(BF16)
    grad_proj = nn_dot(attended_t, out_grad)
    w_proj_pad = jnp.pad(w_proj, ((0, tail), (0, 0)))
    attended_grad = nt_dot(out_grad, w_proj_pad).astype(BF16)

    small = jnp.concatenate([grad_gain_ffn[None], grad_router.T], 0)
    grad_proj, small = sum_groups(grad_proj, small)
    grad_gain_ffn = small[0]
    grad_router = small[1:].T

    stacked_grad, rel_parts = attend_back(proj, kvt[0], lse, attended_grad, rel_bias, head_dim)
    normed1_part = jnp.einsum("tsi,tdi->sd", stacked_grad, w_qkv, preferred_element_type=F32)
    grad_qkv_t = jnp.einsum("tsi,sd->tid", stacked_grad, normed1, preferred_element_type=F32)
    rel_row = jnp.sum(rel_parts, -1).reshape(1, -1)
    rel_row = jnp.pad(rel_row, ((0, 0), (0, width - rel_row.shape[1])))
    grad_qkv_t, rel_row = sum_groups(grad_qkv_t.reshape(3 * inner_here, width), rel_row)
    grad_qkv = jnp.swapaxes(grad_qkv_t.reshape(3, inner_here, width), 1, 2)
    grad_rel = rel_row[0, : rel_bias.size].reshape(rel_bias.shape)
    inverse = lax.rsqrt(jnp.mean(residual * residual, -1, keepdims=True) + 1e-06)

    halves = normed1_part.reshape(2, length // 2, width)
    low_bit = member & 1
    kept = lax.dynamic_index_in_dim(halves, low_bit, 0, False)
    sent = lax.dynamic_index_in_dim(halves, 1 - low_bit, 0, False)
    kept = kept + swap(sent.astype(BF16), 1).astype(F32)
    for bit in bits[1:]:
        kept = kept + swap(kept.astype(BF16), bit).astype(F32)
    kept = kept.astype(BF16)
    other = swap(kept, 1)
    grad_normed1 = jnp.concatenate(
        [jnp.where(low_bit == 0, kept, other), jnp.where(low_bit == 0, other, kept)], 0
    ).astype(F32)
    gain_part = jnp.sum(grad_normed1 * residual * inverse, 0, keepdims=True)
    grad_gain_attn = jnp.sum(gather_groups(gain_part), (0, 1))
    scaled = gain_attn * grad_normed1
    correction = jnp.mean(residual * scaled, -1, keepdims=True)
    grad_input = grad_hidden1 + inverse * scaled - residual * (inverse**3 * correction)
    return (
        output,
        grad_input,
        grad_gain_attn,
        grad_qkv,
        grad_proj,
        grad_rel,
        grad_gain_ffn,
        grad_router,
        grad_w_in[None],
        grad_w_out[None],
    )


def solution(mesh):
    placed = (
        P("expert", None),
        P(),
        P(None, None, "tensor"),
        P("tensor", None),
        P("tensor", None),
        P(),
        P(),
        P("expert", None, "tensor"),
        P("expert", "tensor", None),
        P("expert", None),
        P("expert", None),
        P("expert", None),
    )
    return jax.shard_map(
        shards,
        mesh=mesh,
        in_specs=placed,
        out_specs=(
            P("expert", None),
            P("expert", None),
            P(),
            P(None, None, "tensor"),
            P("tensor", None),
            P("tensor", None),
            P(),
            P(),
            P("expert", None, "tensor"),
            P("expert", "tensor", None),
        ),
        check_vma=False,
    )
```

time: 1020 us -> 477 us (0.47)
  blocking collectives: 324 us -> 0 us
  local copies, waits for them, and re-layouts: 362 us -> 57.8 us
  starting transfers between devices: 9 us -> 139 us
  matrix products: 93.4 us -> 59.1 us
  Pallas kernels: 0 us -> 28.5 us
  waiting for transfers between devices: 169 us -> 154 us
  between operations: 15 us -> 2.33 us
    psum x3 -> x0, blocking collectives: 206 us -> none  [the longest x2 170 us: take_back(): summed = lax.psum(partial_value, 'tensor').astype(jnp.bfloat16)]
    ppermute x0 -> x90, waiting for transfers between devices: none -> 154 us  [the longest x63 95.9 us: across(): return lax.ppermute(value, 'expert', [(i, i ^ k) for i in range(groups)])]
    ppermute x0 -> x90, starting transfers between devices: none -> 139 us  [the longest x63 125 us: across(): return lax.ppermute(value, 'expert', [(i, i ^ k) for i in range(groups)])]
    all_to_all x2 -> x0, blocking collectives: 117 us -> none  [send_rows(): lax.all_to_all(outgoing, 'expert', split_axis=0, concat_axis=0, tiled=True)]
    unnamed x118 -> x178, local copies, waits for them, and re-layouts: 144 us -> 29.3 us
    all_to_all x2 -> x0, waiting for transfers between devices: 97.9 us -> none  [take_back(): lax.all_to_all(summed, 'expert', split_axis=0, concat_axis=0, tiled=True)]
    rev x2 -> x0, local copies, waits for them, and re-layouts: 92.2 us -> none  [diagonal_sums(): flipped = matrix[:, ::-1, :]]
    psum x3 -> x0, waiting for transfers between devices: 70.8 us -> none  [the longest x1 70.7 us: shards(): hidden1 = residual + lax.psum(head_part, 'tensor')]
  transfers between devices with their start and end apart: 5 -> 90, of which waited for: 3 -> 36; matrix products, arithmetic and copies ran while one was open for 25% -> 21% of each run, Pallas kernels for 0% -> 0%
where the time goes in v1:
time: 477 us; the launch traced here: 470 us
  waiting for transfers between devices  154 us (32%)
  starting transfers between devices  139 us (29%)
  matrix products  59.1 us (12%)
  local copies, waits for them, and re-layouts  57.8 us (12%)
  other arithmetic  29.4 us (6%)
  Pallas kernels  28.5 us (6%)
    ppermute x63, starting transfers between devices, across(): return lax.ppermute(value, 'expert', [(i, i ^ k) for i in range(groups)])  125 us
    ppermute x63, waiting for transfers between devices, across(): return lax.ppermute(value, 'expert', [(i, i ^ k) for i in range(groups)])  95.9 us
    ppermute x27, waiting for transfers between devices, swap(): return lax.ppermute(value, 'tensor', [(i, i ^ bit) for i in range(members)])  57.7 us
    unnamed x178, local copies, waits for them, and re-layouts  29.3 us
    dot_general x11, matrix products, nn_dot(): return jnp.dot(left, right, preferred_element_type=F32)  26.2 us
    pallas_call x1, Pallas kernels, attend_back(): pl.pallas_call(functools.partial(attend_back_kernel, length, heads, dim),...  19.5 us
    ppermute x27, starting transfers between devices, swap(): return lax.ppermute(value, 'tensor', [(i, i ^ bit) for i in range(members)])  14.1 us
    dot_general x4, matrix products, nt_dot(): lax.dot_general(left, right, (((1,), (1,)), ((), ())), preferred_element_...  11.4 us
  transfers between devices with their start and end apart: 90, of which 36 were waited for; matrix products, arithmetic and copies ran while one was open for 21% of the time, Pallas kernels for 0%

profile of v1, /device:TPU:0, one launch (start us, length us, event | category | flops | bytes accessed | tf_op | source)
XLA Modules:
  0.0 469.6 jit_solution(15171715565489720282)
XLA Ops:
  0.7 3.0 collective-permute-start.8
  9.7 4.6 collective-permute-start.6
  24.2 3.9 concatenate.45
  28.1 3.4 multiply_add_fusion.proj_ref
  33.6 3.4 collective-permute-done.1
  38.0 4.3 collective-permute-done.2
  44.5 3.9 collective-permute-done.3
  50.6 3.9 collective-permute-done.4
  58.8 9.0 %shard_map.195 = (bf16[192,1024]{1,0:T(8,128)(2,1)S(1)}, f32[8,1024]{1,0:T(8,128)S(1)}) custom-call(bf16[1024,768]{1,0:T(8,128)(2,1)S(1)} %multiply_add_fusion.proj_ref, bf16[192,1024]{1,0:T(8,128)(2,1)S(1)} %get-tuple-element.91.vt_ref, f32[3,32]{1,0:T(4,128)S(1)} %copy-done.2), custom_call_target="tpu_custom_call" | custom-call | flops 805306368 | bytes 4194304 | tf_op jit(solution)/shard_map/pallas_call | solution.py:194
  68.9 11.0 %collective-permute-done.11 = bf16[192,1024]{1,0:T(8,128)(2,1)S(1)} collective-permute-done((bf16[192,1024]{1,0:T(8,128)(2,1)S(1)}, bf16[192,1024]{1,0:T(8,128)(2,1)S(1)}, u32[]{:S(2)}, u32[]{:S(2)}) %collective-permute-start.11) | collective-permute-done | bytes 393248 | tf_op jit(solution)/shard_map/ppermute | solution.py:279
  85.3 3.4 multiply_reduce_fusion
  93.4 3.9 collective-permute-start.19
  98.6 4.7 %collective-permute-done.14 = bf16[48,768]{1,0:T(8,128)(2,1)S(1)} collective-permute-done((bf16[48,768]{1,0:T(8,128)(2,1)S(1)}, bf16[48,768]{1,0:T(8,128)(2,1)S(1)}, u32[]{:S(2)}, u32[]{:S(2)}) %collective-permute-start.14) | collective-permute-done | bytes 73760 | tf_op jit(solution)/shard_map/ppermute | solution.py:302
  103.4 2.9 collective-permute-start.15
  111.0 2.9 collective-permute-done.16
  113.9 3.4 collective-permute-start.17
  117.4 2.7 collective-permute-done.17
  121.9 13.1 %collective-permute-done.24 = bf16[384,768]{1,0:T(8,128)(2,1)S(1)} collective-permute-done((bf16[384,768]{1,0:T(8,128)(2,1)S(1)}, bf16[384,768]{1,0:T(8,128)(2,1)S(1)}, u32[]{:S(2)}, u32[]{:S(2)}) %collective-permute-start.24) | collective-permute-done | bytes 589856 | tf_op jit(solution)/shard_map/ppermute | solution.py:279
  140.1 4.5 fusion.5
  144.6 4.7 %fusion.12 = bf16[1536,768]{1,0:T(8,128)(2,1)S(1)} fusion(f32[1536,768]{1,0:T(8,128)S(1)} %fusion.92, bf16[1536,768]{0,1:T(8,128)(2,1)S(1)} %pad_maximum_fusion, f32[1536]{0:T(1024)S(1)} %multiply_reduce_fusion.1, bf16[1,768,768]{2,1,0:T(8,128)(2,1)S(1)} %copy-done), kind=kOutput, calls=%fused_computation.23 | convolution fusion | flops 1839071232 | bytes 10622976 | tf_op jit(solution)/shard_map/dot_general | solution.py:33
  151.4 3.1 fusion.178
  154.8 3.0 copy.62
  163.4 12.1 %collective-permute-done.28 = bf16[384,768]{1,0:T(8,128)(2,1)S(1)} collective-permute-done((bf16[384,768]{1,0:T(8,128)(2,1)S(1)}, bf16[384,768]{1,0:T(8,128)(2,1)S(1)}, u32[]{:S(2)}, u32[]{:S(2)}) %collective-permute-start.28) | collective-permute-done | bytes 589856 | tf_op jit(solution)/shard_map/ppermute | solution.py:279
  182.3 2.5 collective-permute-start.44
  186.3 2.6 convert.56
  196.9 4.7 collective-permute-done.45
  206.4 12.2 %collective-permute-done.31 = bf16[384,768]{0,1:T(8,128)(2,1)S(1)} collective-permute-done((bf16[384,768]{0,1:T(8,128)(2,1)S(1)}, bf16[384,768]{0,1:T(8,128)(2,1)S(1)}, u32[]{:S(2)}, u32[]{:S(2)}) %collective-permute-start.31) | collective-permute-done | bytes 589856 | tf_op jit(solution)/shard_map/ppermute | solution.py:279
  220.2 3.3 collective-permute-start.38
  225.5 2.6 collective-permute-start.35
  228.0 2.9 collective-permute-done.38
  231.0 15.6 %collective-permute-start.34 = (bf16[48,768]{0,1:T(8,128)(2,1)}, bf16[48,768]{0,1:T(8,128)(2,1)S(1)}, u32[]{:S(2)}, u32[]{:S(2)}) collective-permute-start(bf16[48,768]{0,1:T(8,128)(2,1)} %get-tuple-element.103), channel_id=1, source_target_pairs={{0,12},{4,8},{8,4},{12,0},{16,28},{20,24},{24,20},{28,16},{1,13},{... | collective-permute-start | bytes 221192 | tf_op jit(solution)/shard_map/ppermute | solution.py:302
  246.6 3.4 collective-permute-start.33
  250.0 4.6 collective-permute-done.36
  269.7 7.9 %fusion.58 = f32[1,768,768]{2,1,0:T(8,128)} fusion(bf16[1536,768]{0,1:T(8,128)(2,1)} %copy-done.20, f32[1536]{0:T(1024)S(1)} %multiply_reduce_fusion.1, f32[1536,768]{1,0:T(8,128)} %copy-done.54), kind=kOutput, calls=%fused_computation.78 | convolution fusion | flops 1826095104 | bytes 9443328 | tf_op jit(solution)/shard_map/dot_general | solution.py:436
  277.6 3.5 convolution_bitcast_fusion
  281.6 5.5 %fusion.23 = (bf16[768]{0:T(1024)(128)(2,1)S(1)}, f32[1024]{0:T(1024)S(1)}, bf16[1024,768]{0,1:T(8,128)(2,1)S(1)}) fusion(f32[1024,768]{0,1:T(8,128)S(1)} %copy-done.11, f32[1024]{0:T(1024)S(1)} %fusion.161, f32[768]{0:T(1024)S(1)} %copy-done.42, bf16[384,768]{1,0:T(8,128)(2,1)} %collective-permute-done.51, bf16[384,768]{1,0:T(8,128)(2,1)} %collective-permute-done.50, ...), kind=kOutput, calls=%fused_computation.43 | convolution fusion | flops 2433218816 | bytes 7100928 | tf_op jit(solution)/shard_map/dot_general | solution.py:37
  287.2 3.1 fusion.22
  290.4 2.8 convert_add_fusion.1
  295.8 19.5 %shard_map.196 = (bf16[3,1024,192]{2,1,0:T(8,128)(2,1)}, f32[3,32,128]{2,1,0:T(8,128)}) custom-call(bf16[1024,768]{1,0:T(8,128)(2,1)} %copy-done.3, bf16[192,1024]{1,0:T(8,128)(2,1)} %get-tuple-element.90.kt_ref, f32[8,1024]{1,0:T(8,128)} %copy-done.4, bf16[1024,256]{1,0:T(8,128)(2,1)} %convolution_convert_fusion.1.da_ref, f32[3,32]{1,0:T(4,128)} %bias_ref.3), custom_call_target="tpu_custom_call" | custom-call | flops 2013265920 | bytes 6291456 | tf_op jit(solution)/shard_map/pallas_call | solution.py:218
  315.3 3.2 fusion.71
  327.5 3.8 collective-permute-start.79
  335.7 2.6 copy.69
  339.0 3.0 copy.65
  350.1 3.0 collective-permute-done.83
  353.1 3.5 collective-permute-start.84
  356.7 3.0 collective-permute-done.84
  361.1 3.7 collective-permute-done.85
  366.7 3.1 collective-permute-done.86
  369.9 2.8 collective-permute-start.87
  372.6 3.2 collective-permute-done.87
  375.9 3.6 collective-permute-start.88
  381.9 5.2 %collective-permute-start.89 = (bf16[33,768]{1,0:T(8,128)(2,1)S(1)}, bf16[33,768]{1,0:T(8,128)(2,1)S(1)}, u32[]{:S(2)}, u32[]{:S(2)}) collective-permute-start(bf16[33,768]{1,0:T(8,128)(2,1)S(1)} %pad_maximum_fusion.4), channel_id=1, source_target_pairs={{0,28},{4,24},{8,20},{12,16},{16,12},{20,8},{24,4},{28,0},{1,29},{... | collective-permute-start | bytes 152072 | tf_op jit(solution)/shard_map/ppermute | solution.py:302
  387.1 2.9 collective-permute-done.89
  391.7 4.6 collective-permute-start.64
  407.1 4.2 collective-permute-done.69
  412.1 8.8 %collective-permute-done.70 = bf16[73,768]{1,0:T(8,128)(2,1)S(1)} collective-permute-done((bf16[73,768]{1,0:T(8,128)(2,1)S(1)}, bf16[73,768]{1,0:T(8,128)(2,1)S(1)}, u32[]{:S(2)}, u32[]{:S(2)}) %collective-permute-start.70) | collective-permute-done | bytes 112160 | tf_op jit(solution)/shard_map/ppermute | solution.py:302
  420.9 7.1 %collective-permute-done.71 = bf16[73,768]{1,0:T(8,128)(2,1)S(1)} collective-permute-done((bf16[73,768]{1,0:T(8,128)(2,1)S(1)}, bf16[73,768]{1,0:T(8,128)(2,1)S(1)}, u32[]{:S(2)}, u32[]{:S(2)}) %collective-permute-start.71) | collective-permute-done | bytes 112160 | tf_op jit(solution)/shard_map/ppermute | solution.py:302
  430.1 5.5 %collective-permute-done.75 = bf16[73,768]{1,0:T(8,128)(2,1)S(1)} collective-permute-done((bf16[73,768]{1,0:T(8,128)(2,1)S(1)}, bf16[73,768]{1,0:T(8,128)(2,1)S(1)}, u32[]{:S(2)}, u32[]{:S(2)}) %collective-permute-start.75) | collective-permute-done | bytes 112160 | tf_op jit(solution)/shard_map/ppermute | solution.py:302
  436.7 5.7 %collective-permute-done.53 = bf16[512,768]{0,1:T(8,128)(2,1)S(1)} collective-permute-done((bf16[512,768]{0,1:T(8,128)(2,1)S(1)}, bf16[512,768]{0,1:T(8,128)(2,1)S(1)}, u32[]{:S(2)}, u32[]{:S(2)}) %collective-permute-start.53) | collective-permute-done | bytes 786464 | tf_op jit(solution)/shard_map/ppermute | solution.py:279
  446.1 2.5 convert_bitcast_fusion
  451.4 2.8 collective-permute-start.61
  455.2 3.8 collective-permute-start.58
  462.6 2.4 fusion.18
  465.1 3.5 copy.70
  (426 shorter events, 158.4 us)
Async XLA Ops:
  0.7 53.9 %collective-permute-start.8 = (bf16[192,768]{1,0:T(8,128)(2,1)}, bf16[192,768]{1,0:T(8,128)(2,1)}, u32[]{:S(2)}, u32[]{:S(2)}) collective-permute-start(bf16[192,768]{1,0:T(8,128)(2,1)} %param.15), channel_id=1, source_target_pairs={{0,2},{1,3},{2,0},{3,1},{4,6},{5,7},{6,4},{7,5},{8,10},{9,11},{10,... | collective-permute-start | bytes 884744 | tf_op jit(solution)/shard_map/ppermute | solution.py:279
  3.7 52.7 %collective-permute-start.7 = (bf16[192,768]{1,0:T(8,128)(2,1)}, bf16[192,768]{1,0:T(8,128)(2,1)}, u32[]{:S(2)}, u32[]{:S(2)}) collective-permute-start(bf16[192,768]{1,0:T(8,128)(2,1)} %param.15), channel_id=1, source_target_pairs={{0,1},{1,0},{2,3},{3,2},{4,5},{5,4},{6,7},{7,6},{8,9},{9,8},{10,11... | collective-permute-start | bytes 884744 | tf_op jit(solution)/shard_map/ppermute | solution.py:279
  9.7 45.8 %collective-permute-start.6 = (bf16[48,768]{1,0:T(8,128)(2,1)}, bf16[48,768]{1,0:T(8,128)(2,1)}, u32[]{:S(2)}, u32[]{:S(2)}) collective-permute-start(bf16[48,768]{1,0:T(8,128)(2,1)} %get-tuple-element.114), channel_id=1, source_target_pairs={{0,28},{4,24},{8,20},{12,16},{16,12},{20,8},{24,4},{28,0},{1,29},{... | collective-permute-start | bytes 221192 | tf_op jit(solution)/shard_map/ppermute | solution.py:302
  14.3 40.3 %collective-permute-start.5 = (bf16[48,768]{1,0:T(8,128)(2,1)}, bf16[48,768]{1,0:T(8,128)(2,1)}, u32[]{:S(2)}, u32[]{:S(2)}) collective-permute-start(bf16[48,768]{1,0:T(8,128)(2,1)} %get-tuple-element.115), channel_id=1, source_target_pairs={{0,24},{4,28},{8,16},{12,20},{16,8},{20,12},{24,0},{28,4},{1,25},{... | collective-permute-start | bytes 221192 | tf_op jit(solution)/shard_map/ppermute | solution.py:302
  14.5 18.1 %collective-permute-start = (bf16[48,768]{1,0:T(8,128)(2,1)}, bf16[48,768]{1,0:T(8,128)(2,1)}, u32[]{:S(2)}, u32[]{:S(2)}) collective-permute-start(bf16[48,768]{1,0:T(8,128)(2,1)} %get-tuple-element.120), channel_id=1, source_target_pairs={{0,4},{4,0},{8,12},{12,8},{16,20},{20,16},{24,28},{28,24},{1,5},{5... | collective-permute-start | bytes 221192 | tf_op jit(solution)/shard_map/ppermute | solution.py:302
  48.4 6.2 %collective-permute-start.4 = (bf16[48,768]{1,0:T(8,128)(2,1)S(1)}, bf16[48,768]{1,0:T(8,128)(2,1)S(1)}, u32[]{:S(2)}, u32[]{:S(2)}) collective-permute-start(bf16[48,768]{1,0:T(8,128)(2,1)S(1)} %copy-done.31), channel_id=1, source_target_pairs={{0,20},{4,16},{8,28},{12,24},{16,4},{20,0},{24,12},{28,8},{1,21},{... | collective-permute-start | bytes 221192 | tf_op jit(solution)/shard_map/ppermute | solution.py:302
  68.4 11.5 %collective-permute-start.11 = (bf16[192,1024]{1,0:T(8,128)(2,1)S(1)}, bf16[192,1024]{1,0:T(8,128)(2,1)S(1)}, u32[]{:S(2)}, u32[]{:S(2)}) collective-permute-start(bf16[192,1024]{1,0:T(8,128)(2,1)S(1)} %get-tuple-element.24), channel_id=1, source_target_pairs={{0,2},{1,3},{2,0},{3,1},{4,6},{5,7},{6,4},{7,5},{8,10},{9,11},{10,... | collective-permute-start | bytes 1179656 | tf_op jit(solution)/shard_map/ppermute | solution.py:279
  68.4 11.5 %collective-permute-start.10 = (bf16[192,1024]{1,0:T(8,128)(2,1)S(1)}, bf16[192,1024]{1,0:T(8,128)(2,1)S(1)}, u32[]{:S(2)}, u32[]{:S(2)}) collective-permute-start(bf16[192,1024]{1,0:T(8,128)(2,1)S(1)} %get-tuple-element.24), channel_id=1, source_target_pairs={{0,1},{1,0},{2,3},{3,2},{4,5},{5,4},{6,7},{7,6},{8,9},{9,8},{10,11... | collective-permute-start | bytes 1179656 | tf_op jit(solution)/shard_map/ppermute | solution.py:279
  85.0 32.2 %collective-permute-start.21 = (bf16[384,768]{0,1:T(8,128)(2,1)}, bf16[384,768]{0,1:T(8,128)(2,1)S(1)}, u32[]{:S(2)}, u32[]{:S(2)}) collective-permute-start(bf16[384,768]{0,1:T(8,128)(2,1)} %copy.53), channel_id=1, source_target_pairs={{0,2},{1,3},{2,0},{3,1},{4,6},{5,7},{6,4},{7,5},{8,10},{9,11},{10,... | collective-permute-start | bytes 1769480 | tf_op jit(solution)/shard_map/ppermute | solution.py:279
  85.3 34.8 %collective-permute-start.20 = (bf16[384,768]{0,1:T(8,128)(2,1)}, bf16[384,768]{0,1:T(8,128)(2,1)S(1)}, u32[]{:S(2)}, u32[]{:S(2)}) collective-permute-start(bf16[384,768]{0,1:T(8,128)(2,1)} %copy.53), channel_id=1, source_target_pairs={{0,1},{1,0},{2,3},{3,2},{4,5},{5,4},{6,7},{7,6},{8,9},{9,8},{10,11... | collective-permute-start | bytes 1769480 | tf_op jit(solution)/shard_map/ppermute | solution.py:279
  91.5 6.3 %collective-permute-start.13 = (bf16[48,768]{1,0:T(8,128)(2,1)S(1)}, bf16[48,768]{1,0:T(8,128)(2,1)S(1)}, u32[]{:S(2)}, u32[]{:S(2)}) collective-permute-start(bf16[48,768]{1,0:T(8,128)(2,1)S(1)} %get-tuple-element.113), channel_id=1, source_target_pairs={{0,4},{4,0},{8,12},{12,8},{16,20},{20,16},{24,28},{28,24},{1,5},{5... | collective-permute-start | bytes 221192 | tf_op jit(solution)/shard_map/ppermute | solution.py:302
  93.4 26.6 %collective-permute-start.19 = (bf16[48,768]{1,0:T(8,128)(2,1)S(1)}, bf16[48,768]{1,0:T(8,128)(2,1)S(1)}, u32[]{:S(2)}, u32[]{:S(2)}) collective-permute-start(bf16[48,768]{1,0:T(8,128)(2,1)S(1)} %get-tuple-element.107), channel_id=1, source_target_pairs={{0,28},{4,24},{8,20},{12,16},{16,12},{20,8},{24,4},{28,0},{1,29},{... | collective-permute-start | bytes 221192 | tf_op jit(solution)/shard_map/ppermute | solution.py:302
  97.3 22.8 %collective-permute-start.18 = (bf16[48,768]{1,0:T(8,128)(2,1)S(1)}, bf16[48,768]{1,0:T(8,128)(2,1)S(1)}, u32[]{:S(2)}, u32[]{:S(2)}) collective-permute-start(bf16[48,768]{1,0:T(8,128)(2,1)S(1)} %get-tuple-element.108), channel_id=1, source_target_pairs={{0,24},{4,28},{8,16},{12,20},{16,8},{20,12},{24,0},{28,4},{1,25},{... | collective-permute-start | bytes 221192 | tf_op jit(solution)/shard_map/ppermute | solution.py:302
  120.3 14.7 %collective-permute-start.24 = (bf16[384,768]{1,0:T(8,128)(2,1)S(1)}, bf16[384,768]{1,0:T(8,128)(2,1)S(1)}, u32[]{:S(2)}, u32[]{:S(2)}) collective-permute-start(bf16[384,768]{1,0:T(8,128)(2,1)S(1)} %bitcast.258), channel_id=1, source_target_pairs={{0,2},{1,3},{2,0},{3,1},{4,6},{5,7},{6,4},{7,5},{8,10},{9,11},{10,... | collective-permute-start | bytes 1769480 | tf_op jit(solution)/shard_map/ppermute | solution.py:279
  121.9 13.2 %collective-permute-start.23 = (bf16[384,768]{1,0:T(8,128)(2,1)S(1)}, bf16[384,768]{1,0:T(8,128)(2,1)S(1)}, u32[]{:S(2)}, u32[]{:S(2)}) collective-permute-start(bf16[384,768]{1,0:T(8,128)(2,1)S(1)} %bitcast.259), channel_id=1, source_target_pairs={{0,1},{1,0},{2,3},{3,2},{4,5},{5,4},{6,7},{7,6},{8,9},{9,8},{10,11... | collective-permute-start | bytes 1769480 | tf_op jit(solution)/shard_map/ppermute | solution.py:279
  160.1 15.4 %collective-permute-start.28 = (bf16[384,768]{1,0:T(8,128)(2,1)S(1)}, bf16[384,768]{1,0:T(8,128)(2,1)S(1)}, u32[]{:S(2)}, u32[]{:S(2)}) collective-permute-start(bf16[384,768]{1,0:T(8,128)(2,1)S(1)} %fusion.79), channel_id=1, source_target_pairs={{0,2},{1,3},{2,0},{3,1},{4,6},{5,7},{6,4},{7,5},{8,10},{9,11},{10,... | collective-permute-start | bytes 1769480 | tf_op jit(solution)/shard_map/ppermute | solution.py:279
  177.7 27.6 %collective-permute-start.48 = (bf16[48,768]{1,0:T(8,128)(2,1)S(1)}, bf16[48,768]{1,0:T(8,128)(2,1)S(1)}, u32[]{:S(2)}, u32[]{:S(2)}) collective-permute-start(bf16[48,768]{1,0:T(8,128)(2,1)S(1)} %get-tuple-element.92), channel_id=1, source_target_pairs={{0,28},{4,24},{8,20},{12,16},{16,12},{20,8},{24,4},{28,0},{1,29},{... | collective-permute-start | bytes 221192 | tf_op jit(solution)/shard_map/ppermute | solution.py:302
  179.5 25.1 %collective-permute-start.47 = (bf16[48,768]{1,0:T(8,128)(2,1)S(1)}, bf16[48,768]{1,0:T(8,128)(2,1)S(1)}, u32[]{:S(2)}, u32[]{:S(2)}) collective-permute-start(bf16[48,768]{1,0:T(8,128)(2,1)S(1)} %get-tuple-element.93), channel_id=1, source_target_pairs={{0,24},{4,28},{8,16},{12,20},{16,8},{20,12},{24,0},{28,4},{1,25},{... | collective-permute-start | bytes 221192 | tf_op jit(solution)/shard_map/ppermute | solution.py:302
  181.4 22.5 %collective-permute-start.46 = (bf16[48,768]{1,0:T(8,128)(2,1)S(1)}, bf16[48,768]{1,0:T(8,128)(2,1)S(1)}, u32[]{:S(2)}, u32[]{:S(2)}) collective-permute-start(bf16[48,768]{1,0:T(8,128)(2,1)S(1)} %get-tuple-element.94), channel_id=1, source_target_pairs={{0,20},{4,16},{8,28},{12,24},{16,4},{20,0},{24,12},{28,8},{1,21},{... | collective-permute-start | bytes 221192 | tf_op jit(solution)/shard_map/ppermute | solution.py:302
  182.3 12.1 %collective-permute-start.44 = (bf16[48,768]{1,0:T(8,128)(2,1)S(1)}, bf16[48,768]{1,0:T(8,128)(2,1)S(1)}, u32[]{:S(2)}, u32[]{:S(2)}) collective-permute-start(bf16[48,768]{1,0:T(8,128)(2,1)S(1)} %get-tuple-element.96), channel_id=1, source_target_pairs={{0,12},{4,8},{8,4},{12,0},{16,28},{20,24},{24,20},{28,16},{1,13},{... | collective-permute-start | bytes 221192 | tf_op jit(solution)/shard_map/ppermute | solution.py:302
  193.7 8.4 %collective-permute-start.30 = (bf16[384,768]{0,1:T(8,128)(2,1)S(1)}, bf16[384,768]{0,1:T(8,128)(2,1)S(1)}, u32[]{:S(2)}, u32[]{:S(2)}) collective-permute-start(bf16[384,768]{0,1:T(8,128)(2,1)S(1)} %get-tuple-element.75), channel_id=1, source_target_pairs={{0,1},{1,0},{2,3},{3,2},{4,5},{5,4},{6,7},{7,6},{8,9},{9,8},{10,11... | collective-permute-start | bytes 1769480 | tf_op jit(solution)/shard_map/ppermute | solution.py:279
  194.4 7.2 %collective-permute-start.45 = (bf16[48,768]{1,0:T(8,128)(2,1)S(1)}, bf16[48,768]{1,0:T(8,128)(2,1)S(1)}, u32[]{:S(2)}, u32[]{:S(2)}) collective-permute-start(bf16[48,768]{1,0:T(8,128)(2,1)S(1)} %get-tuple-element.95), channel_id=1, source_target_pairs={{0,16},{4,20},{8,24},{12,28},{16,0},{20,4},{24,8},{28,12},{1,17},{... | collective-permute-start | bytes 221192 | tf_op jit(solution)/shard_map/ppermute | solution.py:302
  202.4 16.2 %collective-permute-start.31 = (bf16[384,768]{0,1:T(8,128)(2,1)S(1)}, bf16[384,768]{0,1:T(8,128)(2,1)S(1)}, u32[]{:S(2)}, u32[]{:S(2)}) collective-permute-start(bf16[384,768]{0,1:T(8,128)(2,1)S(1)} %add_convert_fusion.2), channel_id=1, source_target_pairs={{0,2},{1,3},{2,0},{3,1},{4,6},{5,7},{6,4},{7,5},{8,10},{9,11},{10,... | collective-permute-start | bytes 1769480 | tf_op jit(solution)/shard_map/ppermute | solution.py:279
  205.9 52.2 %collective-permute-start.50 = (bf16[384,768]{1,0:T(8,128)(2,1)}, bf16[384,768]{1,0:T(8,128)(2,1)}, u32[]{:S(2)}, u32[]{:S(2)}) collective-permute-start(bf16[384,768]{1,0:T(8,128)(2,1)} %bitcast.57), channel_id=1, source_target_pairs={{0,2},{1,3},{2,0},{3,1},{4,6},{5,7},{6,4},{7,5},{8,10},{9,11},{10,... | collective-permute-start | bytes 1769480 | tf_op jit(solution)/shard_map/ppermute | solution.py:279
  220.2 10.8 %collective-permute-start.38 = (bf16[48,768]{0,1:T(8,128)(2,1)}, bf16[48,768]{0,1:T(8,128)(2,1)S(1)}, u32[]{:S(2)}, u32[]{:S(2)}) collective-permute-start(bf16[48,768]{0,1:T(8,128)(2,1)} %get-tuple-element.99), channel_id=1, source_target_pairs={{0,28},{4,24},{8,20},{12,16},{16,12},{20,8},{24,4},{28,0},{1,29},{... | collective-permute-start | bytes 221192 | tf_op jit(solution)/shard_map/ppermute | solution.py:302
  223.5 23.1 %collective-permute-start.37 = (bf16[48,768]{0,1:T(8,128)(2,1)}, bf16[48,768]{0,1:T(8,128)(2,1)}, u32[]{:S(2)}, u32[]{:S(2)}) collective-permute-start(bf16[48,768]{0,1:T(8,128)(2,1)} %get-tuple-element.100), channel_id=1, source_target_pairs={{0,24},{4,28},{8,16},{12,20},{16,8},{20,12},{24,0},{28,4},{1,25},{... | collective-permute-start | bytes 221192 | tf_op jit(solution)/shard_map/ppermute | solution.py:302
  225.3 29.3 %collective-permute-start.36 = (bf16[48,768]{0,1:T(8,128)(2,1)}, bf16[48,768]{0,1:T(8,128)(2,1)}, u32[]{:S(2)}, u32[]{:S(2)}) collective-permute-start(bf16[48,768]{0,1:T(8,128)(2,1)} %get-tuple-element.101), channel_id=1, source_target_pairs={{0,20},{4,16},{8,28},{12,24},{16,4},{20,0},{24,12},{28,8},{1,21},{... | collective-permute-start | bytes 221192 | tf_op jit(solution)/shard_map/ppermute | solution.py:302
  225.5 32.7 %collective-permute-start.35 = (bf16[48,768]{0,1:T(8,128)(2,1)}, bf16[48,768]{0,1:T(8,128)(2,1)S(1)}, u32[]{:S(2)}, u32[]{:S(2)}) collective-permute-start(bf16[48,768]{0,1:T(8,128)(2,1)} %get-tuple-element.102), channel_id=1, source_target_pairs={{0,16},{4,20},{8,24},{12,28},{16,0},{20,4},{24,8},{28,12},{1,17},{... | collective-permute-start | bytes 221192 | tf_op jit(solution)/shard_map/ppermute | solution.py:302
  231.0 29.2 %collective-permute-start.34 = (bf16[48,768]{0,1:T(8,128)(2,1)}, bf16[48,768]{0,1:T(8,128)(2,1)S(1)}, u32[]{:S(2)}, u32[]{:S(2)}) collective-permute-start(bf16[48,768]{0,1:T(8,128)(2,1)} %get-tuple-element.103), channel_id=1, source_target_pairs={{0,12},{4,8},{8,4},{12,0},{16,28},{20,24},{24,20},{28,16},{1,13},{... | collective-permute-start | bytes 221192 | tf_op jit(solution)/shard_map/ppermute | solution.py:302
  246.6 15.0 %collective-permute-start.33 = (bf16[48,768]{0,1:T(8,128)(2,1)S(1)}, bf16[48,768]{0,1:T(8,128)(2,1)}, u32[]{:S(2)}, u32[]{:S(2)}) collective-permute-start(bf16[48,768]{0,1:T(8,128)(2,1)S(1)} %get-tuple-element.104), channel_id=1, source_target_pairs={{0,8},{4,12},{8,0},{12,4},{16,24},{20,28},{24,16},{28,20},{1,9},{5... | collective-permute-start | bytes 221192 | tf_op jit(solution)/shard_map/ppermute | solution.py:302
  254.6 8.1 %collective-permute-start.32 = (bf16[48,768]{0,1:T(8,128)(2,1)S(1)}, bf16[48,768]{0,1:T(8,128)(2,1)}, u32[]{:S(2)}, u32[]{:S(2)}) collective-permute-start(bf16[48,768]{0,1:T(8,128)(2,1)S(1)} %get-tuple-element.105), channel_id=1, source_target_pairs={{0,4},{4,0},{8,12},{12,8},{16,20},{20,16},{24,28},{28,24},{1,5},{5... | collective-permute-start | bytes 221192 | tf_op jit(solution)/shard_map/ppermute | solution.py:302
  258.1 23.5 %collective-permute-start.49 = (bf16[384,768]{1,0:T(8,128)(2,1)}, bf16[384,768]{1,0:T(8,128)(2,1)}, u32[]{:S(2)}, u32[]{:S(2)}) collective-permute-start(bf16[384,768]{1,0:T(8,128)(2,1)} %bitcast.57), channel_id=1, source_target_pairs={{0,1},{1,0},{2,3},{3,2},{4,5},{5,4},{6,7},{7,6},{8,9},{9,8},{10,11... | collective-permute-start | bytes 1769480 | tf_op jit(solution)/shard_map/ppermute | solution.py:279
  258.2 23.4 %collective-permute-start.51 = (bf16[384,768]{1,0:T(8,128)(2,1)}, bf16[384,768]{1,0:T(8,128)(2,1)}, u32[]{:S(2)}, u32[]{:S(2)}) collective-permute-start(bf16[384,768]{1,0:T(8,128)(2,1)} %collective-permute-done.50), channel_id=1, source_target_pairs={{0,1},{1,0},{2,3},{3,2},{4,5},{5,4},{6,7},{7,6},{8,9},{9,8},{10,11... | collective-permute-start | bytes 1769480 | tf_op jit(solution)/shard_map/ppermute | solution.py:279
  268.2 13.0 %collective-permute-start.40 = (bf16[384,768]{1,0:T(8,128)(2,1)}, bf16[384,768]{1,0:T(8,128)(2,1)S(1)}, u32[]{:S(2)}, u32[]{:S(2)}) collective-permute-start(bf16[384,768]{1,0:T(8,128)(2,1)} %bitcast.272), channel_id=1, source_target_pairs={{0,2},{1,3},{2,0},{3,1},{4,6},{5,7},{6,4},{7,5},{8,10},{9,11},{10,... | collective-permute-start | bytes 1769480 | tf_op jit(solution)/shard_map/ppermute | solution.py:279
  322.2 10.4 %collective-permute-start.76 = (bf16[24,768]{1,0:T(8,128)(2,1)S(1)}, bf16[24,768]{1,0:T(8,128)(2,1)S(1)}, u32[]{:S(2)}, u32[]{:S(2)}) collective-permute-start(bf16[24,768]{1,0:T(8,128)(2,1)S(1)} %get-tuple-element.121), channel_id=1, source_target_pairs={{0,4},{4,0},{8,12},{12,8},{16,20},{20,16},{24,28},{28,24},{1,5},{5... | collective-permute-start | bytes 110600 | tf_op jit(solution)/shard_map/ppermute | solution.py:302
  323.6 9.1 %collective-permute-start.82 = (bf16[24,768]{1,0:T(8,128)(2,1)S(1)}, bf16[24,768]{1,0:T(8,128)(2,1)S(1)}, u32[]{:S(2)}, u32[]{:S(2)}) collective-permute-start(bf16[24,768]{1,0:T(8,128)(2,1)S(1)} %get-tuple-element.122), channel_id=1, source_target_pairs={{0,28},{4,24},{8,20},{12,16},{16,12},{20,8},{24,4},{28,0},{1,29},{... | collective-permute-start | bytes 110600 | tf_op jit(solution)/shard_map/ppermute | solution.py:302
  325.4 16.9 %collective-permute-start.81 = (bf16[24,768]{1,0:T(8,128)(2,1)}, bf16[24,768]{1,0:T(8,128)(2,1)}, u32[]{:S(2)}, u32[]{:S(2)}) collective-permute-start(bf16[24,768]{1,0:T(8,128)(2,1)} %get-tuple-element.123), channel_id=1, source_target_pairs={{0,24},{4,28},{8,16},{12,20},{16,8},{20,12},{24,0},{28,4},{1,25},{... | collective-permute-start | bytes 110600 | tf_op jit(solution)/shard_map/ppermute | solution.py:302
  327.5 16.3 %collective-permute-start.80 = (bf16[24,768]{1,0:T(8,128)(2,1)}, bf16[24,768]{1,0:T(8,128)(2,1)}, u32[]{:S(2)}, u32[]{:S(2)}) collective-permute-start(bf16[24,768]{1,0:T(8,128)(2,1)} %get-tuple-element.124), channel_id=1, source_target_pairs={{0,20},{4,16},{8,28},{12,24},{16,4},{20,0},{24,12},{28,8},{1,21},{... | collective-permute-start | bytes 110600 | tf_op jit(solution)/shard_map/ppermute | solution.py:302
  327.5 18.1 %collective-permute-start.79 = (bf16[24,768]{1,0:T(8,128)(2,1)}, bf16[24,768]{1,0:T(8,128)(2,1)}, u32[]{:S(2)}, u32[]{:S(2)}) collective-permute-start(bf16[24,768]{1,0:T(8,128)(2,1)} %get-tuple-element.125), channel_id=1, source_target_pairs={{0,16},{4,20},{8,24},{12,28},{16,0},{20,4},{24,8},{28,12},{1,17},{... | collective-permute-start | bytes 110600 | tf_op jit(solution)/shard_map/ppermute | solution.py:302
  332.7 15.1 %collective-permute-start.78 = (bf16[24,768]{1,0:T(8,128)(2,1)}, bf16[24,768]{1,0:T(8,128)(2,1)}, u32[]{:S(2)}, u32[]{:S(2)}) collective-permute-start(bf16[24,768]{1,0:T(8,128)(2,1)} %get-tuple-element.126), channel_id=1, source_target_pairs={{0,12},{4,8},{8,4},{12,0},{16,28},{20,24},{24,20},{28,16},{1,13},{... | collective-permute-start | bytes 110600 | tf_op jit(solution)/shard_map/ppermute | solution.py:302
  332.8 15.0 %collective-permute-start.77 = (bf16[24,768]{1,0:T(8,128)(2,1)S(1)}, bf16[24,768]{1,0:T(8,128)(2,1)}, u32[]{:S(2)}, u32[]{:S(2)}) collective-permute-start(bf16[24,768]{1,0:T(8,128)(2,1)S(1)} %get-tuple-element.127), channel_id=1, source_target_pairs={{0,8},{4,12},{8,0},{12,4},{16,24},{20,28},{24,16},{28,20},{1,9},{5... | collective-permute-start | bytes 110600 | tf_op jit(solution)/shard_map/ppermute | solution.py:302
  342.4 49.4 %collective-permute-start.62 = (bf16[72,768]{1,0:T(8,128)(2,1)}, bf16[72,768]{1,0:T(8,128)(2,1)S(1)}, u32[]{:S(2)}, u32[]{:S(2)}) collective-permute-start(bf16[72,768]{1,0:T(8,128)(2,1)} %get-tuple-element.80), channel_id=1, source_target_pairs={{0,4},{4,0},{8,12},{12,8},{16,20},{20,16},{24,28},{28,24},{1,5},{5... | collective-permute-start | bytes 331784 | tf_op jit(solution)/shard_map/ppermute | solution.py:302
  343.8 52.5 %collective-permute-start.68 = (bf16[72,768]{1,0:T(8,128)(2,1)}, bf16[72,768]{1,0:T(8,128)(2,1)S(1)}, u32[]{:S(2)}, u32[]{:S(2)}) collective-permute-start(bf16[72,768]{1,0:T(8,128)(2,1)} %get-tuple-element.81), channel_id=1, source_target_pairs={{0,28},{4,24},{8,20},{12,16},{16,12},{20,8},{24,4},{28,0},{1,29},{... | collective-permute-start | bytes 331784 | tf_op jit(solution)/shard_map/ppermute | solution.py:302
  345.6 51.3 %collective-permute-start.67 = (bf16[72,768]{1,0:T(8,128)(2,1)}, bf16[72,768]{1,0:T(8,128)(2,1)S(1)}, u32[]{:S(2)}, u32[]{:S(2)}) collective-permute-start(bf16[72,768]{1,0:T(8,128)(2,1)} %get-tuple-element.82), channel_id=1, source_target_pairs={{0,24},{4,28},{8,16},{12,20},{16,8},{20,12},{24,0},{28,4},{1,25},{... | collective-permute-start | bytes 331784 | tf_op jit(solution)/shard_map/ppermute | solution.py:302
  347.7 49.2 %collective-permute-start.66 = (bf16[72,768]{1,0:T(8,128)(2,1)}, bf16[72,768]{1,0:T(8,128)(2,1)S(1)}, u32[]{:S(2)}, u32[]{:S(2)}) collective-permute-start(bf16[72,768]{1,0:T(8,128)(2,1)} %get-tuple-element.83), channel_id=1, source_target_pairs={{0,20},{4,16},{8,28},{12,24},{16,4},{20,0},{24,12},{28,8},{1,21},{... | collective-permute-start | bytes 331784 | tf_op jit(solution)/shard_map/ppermute | solution.py:302
  353.1 6.5 %collective-permute-start.84 = (bf16[33,768]{1,0:T(8,128)(2,1)S(1)}, bf16[33,768]{1,0:T(8,128)(2,1)S(1)}, u32[]{:S(2)}, u32[]{:S(2)}) collective-permute-start(bf16[33,768]{1,0:T(8,128)(2,1)S(1)} %pad_maximum_fusion.4), channel_id=1, source_target_pairs={{0,8},{4,12},{8,0},{12,4},{16,24},{20,28},{24,16},{28,20},{1,9},{5... | collective-permute-start | bytes 152072 | tf_op jit(solution)/shard_map/ppermute | solution.py:302
  381.9 8.0 %collective-permute-start.89 = (bf16[33,768]{1,0:T(8,128)(2,1)S(1)}, bf16[33,768]{1,0:T(8,128)(2,1)S(1)}, u32[]{:S(2)}, u32[]{:S(2)}) collective-permute-start(bf16[33,768]{1,0:T(8,128)(2,1)S(1)} %pad_maximum_fusion.4), channel_id=1, source_target_pairs={{0,28},{4,24},{8,20},{12,16},{16,12},{20,8},{24,4},{28,0},{1,29},{... | collective-permute-start | bytes 152072 | tf_op jit(solution)/shard_map/ppermute | solution.py:302
  390.0 7.0 %collective-permute-start.65 = (bf16[72,768]{1,0:T(8,128)(2,1)}, bf16[72,768]{1,0:T(8,128)(2,1)S(1)}, u32[]{:S(2)}, u32[]{:S(2)}) collective-permute-start(bf16[72,768]{1,0:T(8,128)(2,1)} %get-tuple-element.84), channel_id=1, source_target_pairs={{0,16},{4,20},{8,24},{12,28},{16,0},{20,4},{24,8},{28,12},{1,17},{... | collective-permute-start | bytes 331784 | tf_op jit(solution)/shard_map/ppermute | solution.py:302
  391.7 7.3 %collective-permute-start.64 = (bf16[72,768]{1,0:T(8,128)(2,1)S(1)}, bf16[72,768]{1,0:T(8,128)(2,1)S(1)}, u32[]{:S(2)}, u32[]{:S(2)}) collective-permute-start(bf16[72,768]{1,0:T(8,128)(2,1)S(1)} %copy-done.30), channel_id=1, source_target_pairs={{0,12},{4,8},{8,4},{12,0},{16,28},{20,24},{24,20},{28,16},{1,13},{... | collective-permute-start | bytes 331784 | tf_op jit(solution)/shard_map/ppermute | solution.py:302
  396.9 31.2 %collective-permute-start.52 = (bf16[512,768]{0,1:T(8,128)(2,1)S(1)}, bf16[512,768]{0,1:T(8,128)(2,1)S(1)}, u32[]{:S(2)}, u32[]{:S(2)}) collective-permute-start(bf16[512,768]{0,1:T(8,128)(2,1)S(1)} %bitcast.257), channel_id=1, source_target_pairs={{0,1},{1,0},{2,3},{3,2},{4,5},{5,4},{6,7},{7,6},{8,9},{9,8},{10,11... | collective-permute-start | bytes 2359304 | tf_op jit(solution)/shard_map/ppermute | solution.py:279
  402.1 26.0 %collective-permute-start.74 = (bf16[73,768]{1,0:T(8,128)(2,1)S(1)}, bf16[73,768]{1,0:T(8,128)(2,1)S(1)}, u32[]{:S(2)}, u32[]{:S(2)}) collective-permute-start(bf16[73,768]{1,0:T(8,128)(2,1)S(1)} %fusion.109), channel_id=1, source_target_pairs={{0,24},{4,28},{8,16},{12,20},{16,8},{20,12},{24,0},{28,4},{1,25},{... | collective-permute-start | bytes 336392 | tf_op jit(solution)/shard_map/ppermute | solution.py:302
  402.7 25.3 %collective-permute-start.73 = (bf16[73,768]{1,0:T(8,128)(2,1)S(1)}, bf16[73,768]{1,0:T(8,128)(2,1)S(1)}, u32[]{:S(2)}, u32[]{:S(2)}) collective-permute-start(bf16[73,768]{1,0:T(8,128)(2,1)S(1)} %fusion.109), channel_id=1, source_target_pairs={{0,20},{4,16},{8,28},{12,24},{16,4},{20,0},{24,12},{28,8},{1,21},{... | collective-permute-start | bytes 336392 | tf_op jit(solution)/shard_map/ppermute | solution.py:302
  404.8 23.2 %collective-permute-start.72 = (bf16[73,768]{1,0:T(8,128)(2,1)S(1)}, bf16[73,768]{1,0:T(8,128)(2,1)S(1)}, u32[]{:S(2)}, u32[]{:S(2)}) collective-permute-start(bf16[73,768]{1,0:T(8,128)(2,1)S(1)} %fusion.109), channel_id=1, source_target_pairs={{0,16},{4,20},{8,24},{12,28},{16,0},{20,4},{24,8},{28,12},{1,17},{... | collective-permute-start | bytes 336392 | tf_op jit(solution)/shard_map/ppermute | solution.py:302
  411.4 9.5 %collective-permute-start.70 = (bf16[73,768]{1,0:T(8,128)(2,1)S(1)}, bf16[73,768]{1,0:T(8,128)(2,1)S(1)}, u32[]{:S(2)}, u32[]{:S(2)}) collective-permute-start(bf16[73,768]{1,0:T(8,128)(2,1)S(1)} %fusion.109), channel_id=1, source_target_pairs={{0,8},{4,12},{8,0},{12,4},{16,24},{20,28},{24,16},{28,20},{1,9},{5... | collective-permute-start | bytes 336392 | tf_op jit(solution)/shard_map/ppermute | solution.py:302
  420.9 7.1 %collective-permute-start.71 = (bf16[73,768]{1,0:T(8,128)(2,1)S(1)}, bf16[73,768]{1,0:T(8,128)(2,1)S(1)}, u32[]{:S(2)}, u32[]{:S(2)}) collective-permute-start(bf16[73,768]{1,0:T(8,128)(2,1)S(1)} %fusion.109), channel_id=1, source_target_pairs={{0,12},{4,8},{8,4},{12,0},{16,28},{20,24},{24,20},{28,16},{1,13},{... | collective-permute-start | bytes 336392 | tf_op jit(solution)/shard_map/ppermute | solution.py:302
  428.0 7.6 %collective-permute-start.75 = (bf16[73,768]{1,0:T(8,128)(2,1)S(1)}, bf16[73,768]{1,0:T(8,128)(2,1)S(1)}, u32[]{:S(2)}, u32[]{:S(2)}) collective-permute-start(bf16[73,768]{1,0:T(8,128)(2,1)S(1)} %fusion.109), channel_id=1, source_target_pairs={{0,28},{4,24},{8,20},{12,16},{16,12},{20,8},{24,4},{28,0},{1,29},{... | collective-permute-start | bytes 336392 | tf_op jit(solution)/shard_map/ppermute | solution.py:302
  428.4 14.0 %collective-permute-start.53 = (bf16[512,768]{0,1:T(8,128)(2,1)S(1)}, bf16[512,768]{0,1:T(8,128)(2,1)S(1)}, u32[]{:S(2)}, u32[]{:S(2)}) collective-permute-start(bf16[512,768]{0,1:T(8,128)(2,1)S(1)} %fusion.96), channel_id=1, source_target_pairs={{0,2},{1,3},{2,0},{3,1},{4,6},{5,7},{6,4},{7,5},{8,10},{9,11},{10,... | collective-permute-start | bytes 2359304 | tf_op jit(solution)/shard_map/ppermute | solution.py:279
  451.4 8.1 %collective-permute-start.61 = (f32[1,768]{1,0:T(1,128)S(1)}, f32[1,768]{1,0:T(1,128)S(1)}, u32[]{:S(2)}, u32[]{:S(2)}) collective-permute-start(f32[1,768]{1,0:T(1,128)S(1)} %broadcast_in_dim.36), channel_id=1, source_target_pairs={{0,28},{4,24},{8,20},{12,16},{16,12},{20,8},{24,4},{28,0},{1,29},{... | collective-permute-start | bytes 9224 | tf_op jit(solution)/shard_map/ppermute | solution.py:302
  454.1 7.0 %collective-permute-start.60 = (f32[1,768]{1,0:T(1,128)S(1)}, f32[1,768]{1,0:T(1,128)S(1)}, u32[]{:S(2)}, u32[]{:S(2)}) collective-permute-start(f32[1,768]{1,0:T(1,128)S(1)} %broadcast_in_dim.36), channel_id=1, source_target_pairs={{0,24},{4,28},{8,16},{12,20},{16,8},{20,12},{24,0},{28,4},{1,25},{... | collective-permute-start | bytes 9224 | tf_op jit(solution)/shard_map/ppermute | solution.py:302
  455.2 13.4 %collective-permute-start.59 = (f32[1,768]{1,0:T(1,128)S(1)}, f32[1,768]{1,0:T(1,128)S(1)}, u32[]{:S(2)}, u32[]{:S(2)}) collective-permute-start(f32[1,768]{1,0:T(1,128)S(1)} %broadcast_in_dim.36), channel_id=1, source_target_pairs={{0,20},{4,16},{8,28},{12,24},{16,4},{20,0},{24,12},{28,8},{1,21},{... | collective-permute-start | bytes 9224 | tf_op jit(solution)/shard_map/ppermute | solution.py:302
  455.2 13.4 %collective-permute-start.58 = (f32[1,768]{1,0:T(1,128)S(1)}, f32[1,768]{1,0:T(1,128)S(1)}, u32[]{:S(2)}, u32[]{:S(2)}) collective-permute-start(f32[1,768]{1,0:T(1,128)S(1)} %broadcast_in_dim.36), channel_id=1, source_target_pairs={{0,16},{4,20},{8,24},{12,28},{16,0},{20,4},{24,8},{28,12},{1,17},{... | collective-permute-start | bytes 9224 | tf_op jit(solution)/shard_map/ppermute | solution.py:302
  459.1 9.7 %collective-permute-start.57 = (f32[1,768]{1,0:T(1,128)S(1)}, f32[1,768]{1,0:T(1,128)S(1)}, u32[]{:S(2)}, u32[]{:S(2)}) collective-permute-start(f32[1,768]{1,0:T(1,128)S(1)} %broadcast_in_dim.36), channel_id=1, source_target_pairs={{0,12},{4,8},{8,4},{12,0},{16,28},{20,24},{24,20},{28,16},{1,13},{... | collective-permute-start | bytes 9224 | tf_op jit(solution)/shard_map/ppermute | solution.py:302
  459.4 9.3 %collective-permute-start.56 = (f32[1,768]{1,0:T(1,128)S(1)}, f32[1,768]{1,0:T(1,128)S(1)}, u32[]{:S(2)}, u32[]{:S(2)}) collective-permute-start(f32[1,768]{1,0:T(1,128)S(1)} %broadcast_in_dim.36), channel_id=1, source_target_pairs={{0,8},{4,12},{8,0},{12,4},{16,24},{20,28},{24,16},{28,20},{1,9},{5... | collective-permute-start | bytes 9224 | tf_op jit(solution)/shard_map/ppermute | solution.py:302
  461.2 7.6 %collective-permute-start.55 = (f32[1,768]{1,0:T(1,128)S(1)}, f32[1,768]{1,0:T(1,128)S(1)}, u32[]{:S(2)}, u32[]{:S(2)}) collective-permute-start(f32[1,768]{1,0:T(1,128)S(1)} %broadcast_in_dim.36), channel_id=1, source_target_pairs={{0,4},{4,0},{8,12},{12,8},{16,20},{20,16},{24,28},{28,24},{1,5},{5... | collective-permute-start | bytes 9224 | tf_op jit(solution)/shard_map/ppermute | solution.py:302
  (85 other events, 888.8 us)
